TPU v7x, 32 devices: a whole 2x2x4 slice. The times are simulated.
32 devices in a mesh: seq: 16 (over z, y, x), head: 2 (over core).
Axes of the slice: x: 2, y: 2, z: 4, core: 2. Of those that a mesh axis runs over, the one named last changes fastest.
Arguments:
- inputs: bfloat16 [8192, 4096], P('seq', 'head'), may hold values from -6 to 6
- latent: float32 [4096, 512], P('seq', 'head'), as said below
- queries: bfloat16 [8192, 512], P('seq', 'head'), may hold values from -6 to 6
- keys: bfloat16 [8192, 512], P('seq', 'head'), may hold values from -6 to 6
- grad_out: bfloat16 [8192, 512], P('seq', 'head'), may hold values from -6 to 6
Outputs:
- attn_out: bfloat16 [8192, 512], P('seq', 'head')
- grad_queries: bfloat16 [8192, 512], P('seq', 'head')
- grad_keys: bfloat16 [8192, 512], P('seq', 'head')
- grad_latent: float32 [4096, 512], P('seq', 'head')
Inputs may be any that keep to these rules, and one draw needn't show every extreme that they name: `latent`: no entry's magnitude lies between 0.67 and 1.5 times half of its column's mean magnitude.
All inputs are finite; a program needn't handle non-finite values.
Results may differ from a plain program's by a relative error of at most 0.014.
Values may be sent and summed in bfloat16 or wider, within the bound.
No kernel may reach another device: no remote copies, remote signals or barrier semaphores. Data moves between devices by JAX's collectives and lax.ppermute only.
A program may use at most 64 MiB of HBM per device.

v0:
```python
import jax
import jax.numpy as jnp
from jax import lax
from jax.sharding import PartitionSpec as P

DK = 128
BLOCK = 128


absmean_eps = 1e-05
norm_eps = 1e-06


def entering(array, axis, join, neutral, backward):
    count = lax.axis_size(axis)
    place = lax.axis_index(axis)
    ahead = count - 1 - place if backward else place
    gathered = lax.all_gather(array.astype(jnp.bfloat16), axis)
    state = jnp.zeros_like(array) + jnp.asarray(neutral, array.dtype)

    def one(turn, state):
        source = count - 1 - turn if backward else turn
        return join(state, lax.dynamic_index_in_dim(gathered, source, 0, False).astype(array.dtype))

    return lax.fori_loop(0, ahead, one, state)


def ternarize(weights, column_scale):
    halfway = 0.5 * column_scale
    ternary_signs = jnp.where(weights > halfway, 1.0, jnp.where(weights < -halfway, -1.0, 0.0))
    return (ternary_signs * column_scale).astype(jnp.bfloat16)


def blocked(matrix, head_count):
    return matrix.reshape(matrix.shape[0] // BLOCK, BLOCK, head_count, DK)


def add_states(earlier, follows):
    return earlier + follows


def split_pair(state):
    upper = state.astype(jnp.bfloat16)
    lower = (state - upper.astype(jnp.float32)).astype(jnp.bfloat16)
    return (upper, lower)


def state_product(form, operand, state_pair):
    first = jnp.einsum(form, operand, state_pair[0], preferred_element_type=jnp.float32)
    return first + jnp.einsum(form, operand, state_pair[1], preferred_element_type=jnp.float32)


def per_device(inputs, latent, queries, keys, grad_out):
    columns = latent.shape[1]
    head_count = columns // DK
    tokens = inputs.shape[0]
    features_all = lax.all_gather(inputs, "head", axis=1, tiled=True)
    total_rows = latent.shape[0] * lax.axis_size("seq")
    column_sums = lax.psum(jnp.sum(jnp.abs(latent), axis=0), "seq")
    column_scale = column_sums / total_rows + absmean_eps
    projected = jnp.dot(
        features_all,
        ternarize(
            lax.all_gather(latent.astype(jnp.bfloat16), "seq", axis=0, tiled=True).astype(
                jnp.float32
            ),
            column_scale,
        ),
        preferred_element_type=jnp.float32,
    )
    query_blocks = blocked(queries, head_count)
    key_blocks = blocked(keys, head_count)
    value_blocks = blocked(projected.astype(jnp.bfloat16), head_count)
    causal = jnp.tril(jnp.ones((BLOCK, BLOCK), jnp.bool_))
    scores = jnp.where(
        causal,
        jnp.einsum("bthd,bshd->bhts", query_blocks, key_blocks, preferred_element_type=jnp.float32),
        0.0,
    ).astype(jnp.bfloat16)
    within = jnp.einsum("bhts,bshd->bthd", scores, value_blocks, preferred_element_type=jnp.float32)
    block_states = jnp.einsum(
        "bshd,bshe->bhde", key_blocks, value_blocks, preferred_element_type=jnp.float32
    )
    local_total = jnp.sum(block_states, axis=0)
    incoming = entering(local_total, "seq", add_states, jnp.zeros_like(local_total), False)
    prior = incoming[None] + (jnp.cumsum(block_states, axis=0) - block_states)
    prior_pair = split_pair(prior)
    across = state_product("bthd,bhde->bthe", query_blocks, prior_pair)
    mixed = within + across
    root_mean = jnp.sqrt(jnp.mean(mixed * mixed, axis=-1, keepdims=True) + norm_eps)
    normed = mixed / root_mean
    attn_out = normed.astype(jnp.bfloat16).reshape(tokens, columns)
    upstream = blocked(grad_out, head_count).astype(jnp.float32)
    inner_mean = jnp.mean(upstream * normed, axis=-1, keepdims=True)
    grad_mixed = ((upstream - normed * inner_mean) / root_mean).astype(jnp.bfloat16)
    grad_states = jnp.einsum(
        "bthd,bthe->bhde", query_blocks, grad_mixed, preferred_element_type=jnp.float32
    )
    grad_total = jnp.sum(grad_states, axis=0)
    arriving = entering(grad_total, "seq", add_states, jnp.zeros_like(grad_total), True)
    following = arriving[None] + (grad_total[None] - jnp.cumsum(grad_states, axis=0))
    following_pair = split_pair(following)
    grad_scores = jnp.where(
        causal,
        jnp.einsum("bthe,bshe->bhts", grad_mixed, value_blocks, preferred_element_type=jnp.float32),
        0.0,
    ).astype(jnp.bfloat16)
    grad_query = jnp.einsum(
        "bhts,bshd->bthd", grad_scores, key_blocks, preferred_element_type=jnp.float32
    ) + state_product("bthe,bhde->bthd", grad_mixed, prior_pair)
    grad_key = jnp.einsum(
        "bhts,bthd->bshd", grad_scores, query_blocks, preferred_element_type=jnp.float32
    ) + state_product("bshe,bhde->bshd", value_blocks, following_pair)
    grad_value = jnp.einsum(
        "bhts,bthe->bshe", scores, grad_mixed, preferred_element_type=jnp.float32
    ) + state_product("bshd,bhde->bshe", key_blocks, following_pair)
    grad_flat = grad_value.astype(jnp.bfloat16).reshape(tokens, columns)
    weight_term = lax.dot_general(
        features_all, grad_flat, (((0,), (0,)), ((), ())), preferred_element_type=jnp.float32
    )
    grad_latent = lax.psum_scatter(weight_term, "seq", scatter_dimension=0, tiled=True)
    grad_queries = grad_query.astype(jnp.bfloat16).reshape(tokens, columns)
    grad_keys = grad_key.astype(jnp.bfloat16).reshape(tokens, columns)
    return (attn_out, grad_queries, grad_keys, grad_latent)


def solution(mesh):
    placed = (
        P("seq", "head"),
        P("seq", "head"),
        P("seq", "head"),
        P("seq", "head"),
        P("seq", "head"),
    )
    return jax.shard_map(
        per_device,
        mesh=mesh,
        in_specs=placed,
        out_specs=(P("seq", "head"), P("seq", "head"), P("seq", "head"), P("seq", "head")),
        check_vma=False,
    )
```

profile of v0, /device:TPU:0, one launch (start us, length us, event | category | flops | bytes accessed | tf_op | source)
XLA Modules:
  0.0 341.1 jit_solution(18352776995469250471)
XLA Ops:
  7.2 1.7 abs_reduce_fusion
  9.7 1.0 reshape.72
  10.8 43.7 %psum.7 = f32[256]{0:T(256)S(1)} all-reduce(f32[256]{0:T(256)S(1)} %get-tuple-element.119), channel_id=1, replica_groups=mesh['seq'=16,'head'=2] {'seq'}, use_global_device_ids=true, to_apply=%region_1.0 | all-reduce | flops 256 | bytes 2048 | tf_op jit(solution)/shard_map/psum | solution.py:59
  54.4 20.6 %all-gather.7.cloned.1.call-done = bf16[4096,256]{1,0:T(8,128)(2,1)} async-done(((bf16[256,256]{1,0:T(8,128)(2,1)}), bf16[4096,256]{1,0:T(8,128)(2,1)}) %all-gather.7.cloned.1.call-update) | async-done | bytes 2097168 | tf_op jit(solution)/shard_map/all_gather | solution.py:64
  75.0 13.9 %all-gather.9.cloned.1.call-done = bf16[512,4096]{1,0:T(8,128)(2,1)} async-done(((bf16[512,2048]{1,0:T(8,128)(2,1)}), bf16[512,4096]{1,0:T(8,128)(2,1)}) %all-gather.9.cloned.1.call-update) | async-done | bytes 4194320 | tf_op jit(solution)/shard_map/all_gather | solution.py:57
  88.9 4.2 %fusion.22 = bf16[512,256]{0,1:T(8,128)(2,1)S(1)} fusion(bf16[512,4096]{1,0:T(8,128)(2,1)} %all-gather.9.cloned.1.call-done, bf16[4096,256]{1,0:T(8,128)(2,1)} %all-gather.7.cloned.1.call-done, f32[256]{0:T(256)S(1)} %get-tuple-element.123, f32[256]{0:T(256)S(1)} %get-tuple-element.122, f32[256]{0:T(256)S(1)} %get-tuple-element.121), kind=kOutput, calls=%fused_computation.40 | convolution fusion | flops 1081212928 | bytes 6556672 | tf_op jit(solution)/shard_map/dot_general | solution.py:61
  93.7 0.7 copy.120
  95.7 55.3 %all-gather.11.cloned.1.call-done = bf16[32,128,128]{2,1,0:T(8,128)(2,1)} async-done(((bf16[2,128,128]{2,1,0:T(8,128)(2,1)}), bf16[32,128,128]{2,1,0:T(8,128)(2,1)}) %all-gather.11.cloned.1.call-update) | async-done | bytes 1048592 | tf_op jit(solution)/shard_map/all_gather | solution.py:18
  152.1 0.8 divide_convert_fusion
  153.2 0.7 copy.140
  154.2 67.2 %all-gather.13.cloned.1.call-done = bf16[32,128,128]{2,1,0:T(8,128)(2,1)} async-done(((bf16[2,128,128]{2,1,0:T(8,128)(2,1)}), bf16[32,128,128]{2,1,0:T(8,128)(2,1)}) %all-gather.13.cloned.1.call-update) | async-done | bytes 1048592 | tf_op jit(solution)/shard_map/all_gather | solution.py:18
  221.4 13.3 %while.23 = (s32[]{:T(128)}, f32[2,128,128]{2,1,0:T(8,128)S(1)}, s32[]{:T(128)}, bf16[16,2,128,128]{3,2,1,0:T(8,128)(2,1)}, s32[]{:T(128)}, /*index=5*/s32[]{:T(128)}, s32[]{:T(128)}, s32[]{:T(128)}) while((s32[]{:T(128)}, f32[2,128,128]{2,1,0:T(8,128)S(1)}, s32[]{:T(128)}, bf16[16,2,128,128]{3,2,1,0:T(8,128)(2,1)}, s32[]{:T(128)}, ...), condition=%wide.region_10.11_spmd, body=%wide.region_9.10_spmd.sunk | while | flops 65542 | bytes 327823 | solution.py:25
  221.5 0.9 convert_add_fusion.5
  222.4 0.9 convert_add_fusion.5
  223.2 0.9 convert_add_fusion.5
  224.1 0.9 convert_add_fusion.5
  225.0 0.9 convert_add_fusion.5
  225.9 0.9 convert_add_fusion.5
  226.8 0.9 convert_add_fusion.5
  227.7 0.9 convert_add_fusion.5
  228.6 0.9 convert_add_fusion.5
  229.5 0.9 convert_add_fusion.5
  230.3 0.9 convert_add_fusion.5
  231.2 0.9 convert_add_fusion.5
  232.1 0.9 convert_add_fusion.5
  233.0 0.9 convert_add_fusion.5
  233.9 0.9 convert_add_fusion.5
  235.8 5.4 %convolution_bitcast_fusion = f32[4096,256]{0,1:T(8,128)} fusion(bf16[512,4096]{1,0:T(8,128)(2,1)} %all-gather.9.cloned.1.call-done, bf16[64,8,2,128]{3,2,1,0:T(2,128)(2,1)S(1)} %bitcast.78), kind=kOutput, calls=%fused_computation.2 | convolution fusion | flops 1073741824 | bytes 8650752 | tf_op jit(solution)/shard_map/dot_general | solution.py:118
  241.2 0.9 copy-done
  245.5 0.9 copy_bitcast_fusion
  246.4 86.4 %reduce-scatter.2.cloned.1.call-done = f32[256,256]{0,1:T(8,128)} async-done(((f32[4096,256]{0,1:T(8,128)}), f32[256,256]{0,1:T(8,128)}) %reduce-scatter.2.cloned.1.call-update) | async-done | bytes 262160 | tf_op jit(solution)/shard_map/reduce_scatter | solution.py:121
  332.8 1.8 copy.152
  (54 shorter events, 8.4 us)
Async XLA Ops:
  7.2 67.8 %all-gather.7.cloned.1.call-start = ((), (), s32[]{:S(2)}) async-start(), calls=%async_computation.1 | async-start | bytes 2228224 | tf_op jit(solution)/shard_map/all_gather | solution.py:64
  8.9 80.0 %all-gather.9.cloned.1.call-start = ((), (), s32[]{:S(2)}) async-start(), calls=%async_computation.2 | async-start | bytes 6291456 | tf_op jit(solution)/shard_map/all_gather | solution.py:57
  9.7 141.4 %all-gather.11.cloned.1.call-start = ((), (), s32[]{:S(2)}) async-start(), calls=%async_computation.4 | async-start | bytes 1114112 | tf_op jit(solution)/shard_map/all_gather | solution.py:18
  88.9 5.6 %copy-start.1 = (bf16[512,256]{1,0:T(8,128)(2,1)S(1)}, bf16[512,256]{1,0:T(8,128)(2,1)}, u32[]{:S(2)}) copy-start(bf16[512,256]{1,0:T(8,128)(2,1)} %param.13) | copy-start | bytes 786436
  93.1 1.9 copy-start.2
  94.5 127.0 %all-gather.13.cloned.1.call-start = ((), (), s32[]{:S(2)}) async-start(), calls=%async_computation.5 | async-start | bytes 1114112 | tf_op jit(solution)/shard_map/all_gather | solution.py:18
  153.9 178.8 %reduce-scatter.2.cloned.1.call-start = ((), (), s32[]{:S(2)}) async-start(), calls=%async_computation.3 | async-start | bytes 4456448 | tf_op jit(solution)/shard_map/reduce_scatter | solution.py:121
  241.2 0.9 copy-start
Sparse Core Ops, SparseCore 0:
  11.3 63.6 all-gather.6
  76.6 12.3 all-gather.8
  94.6 56.4 all-gather.10
  154.2 67.1 all-gather.12
  241.4 91.3 reduce-scatter.1
where the time goes:
time: 342 us; the launch traced here: 341 us
  waiting for transfers between devices  244 us (71%)
  blocking collectives  43.7 us (13%)
  other arithmetic  15.9 us (5%)
  matrix products  14 us (4%)
  between operations  14 us (4%)
  local copies, waits for them, and re-layouts  8.71 us (3%)
    all_gather x2, waiting for transfers between devices, entering(): gathered = lax.all_gather(array.astype(jnp.bfloat16), axis)  123 us
    reduce_scatter x1, waiting for transfers between devices, per_device(): lax.psum_scatter(weight_term, 'seq', scatter_dimension=0, tiled=True)  86.4 us
    psum x1, blocking collectives, per_device(): column_sums = lax.psum(jnp.sum(jnp.abs(latent), axis=0), 'seq')  43.7 us
    all_gather x1, waiting for transfers between devices, per_device(): lax.all_gather(latent.astype(jnp.bfloat16), 'seq', axis=0, tiled=True)  20.6 us
    all_gather x1, waiting for transfers between devices, per_device(): features_all = lax.all_gather(inputs, 'head', axis=1, tiled=True)  13.9 us
    add x15, other arithmetic, add_states(): return earlier + follows  13 us
  transfers between devices with their start and end apart: 5, of which 5 were waited for; matrix products, arithmetic and copies ran while one was open for 2% of the time, Pallas kernels for 0%

commit v1 on v0

v1 whole, which is shorter than its diff:
```python
import functools

import jax
import jax.numpy as jnp
from jax import lax
from jax.experimental import pallas as pl
from jax.experimental.pallas import tpu as pltpu
from jax.sharding import PartitionSpec as P

DK = 128
BLOCK = 128

absmean_eps = 1e-05
norm_eps = 1e-06

BF16 = jnp.bfloat16
F32 = jnp.float32
VMEM_LIMIT = 48 * 1024 * 1024


def rows_by_rows(a, b):
    return lax.dot_general(a, b, (((0,), (0,)), ((), ())), preferred_element_type=F32)


def by_rows(a, b):
    return lax.dot_general(a, b, (((1,), (1,)), ((), ())), preferred_element_type=F32)


def plain(a, b):
    return jnp.dot(a, b, preferred_element_type=F32)


def block_rows(i):
    return slice(i * BLOCK, (i + 1) * BLOCK)


def causal_mask():
    at = lax.broadcasted_iota(jnp.int32, (BLOCK, BLOCK), 0)
    of = lax.broadcasted_iota(jnp.int32, (BLOCK, BLOCK), 1)
    return at >= of


def place():
    s = lax.axis_index("seq")
    return lax.rem(s, 2), lax.div(s, 2), lax.axis_index("head")


def swap(array, axis, distance):
    count = lax.axis_size(axis)
    return lax.ppermute(array, axis, [(i, i ^ distance) for i in range(count)])


def project_kernel(slabs, heads, total_rows, *refs):
    slab_refs = refs[:slabs]
    sums_ref = refs[slabs]
    piece_refs = refs[slabs + 1 : slabs + 1 + 2 * heads]
    keep_ref, send_ref, x_ref, w_ref, sems = refs[slabs + 1 + 2 * heads :]
    side, pair, head = place()
    tokens, width = piece_refs[0].shape
    rows = slab_refs[0].shape[0]
    copies = []
    for k in range(heads):
        for t in range(2):
            at = pl.multiple_of((side ^ t) * tokens, tokens)
            lane = pl.multiple_of((head ^ k) * width, width)
            copy = pltpu.make_async_copy(
                piece_refs[2 * k + t],
                x_ref.at[pl.ds(at, tokens), pl.ds(lane, width)],
                sems.at[2 * k + t],
            )
            copy.start()
            copies.append(copy)
    scale = jnp.sum(sums_ref[...], axis=0, keepdims=True) / total_rows + absmean_eps
    halfway = 0.5 * scale
    for r in range(slabs):
        w = slab_refs[r][...].astype(F32)
        signs = jnp.where(w > halfway, scale, jnp.where(w < -halfway, -scale, 0.0))
        w_ref[pl.ds(pl.multiple_of((pair ^ r) * rows, rows), rows), :] = signs.astype(BF16)
    for copy in copies:
        copy.wait()
    step = 2 * BLOCK

    def one(i, carry):
        at = pl.ds(pl.multiple_of(i * step, step), step)
        p = plain(x_ref[at, :], w_ref[...])
        own = jnp.where(side == 0, p[:, :DK], p[:, DK:])
        other = jnp.where(side == 0, p[:, DK:], p[:, :DK])
        keep_ref[at, :] = own
        send_ref[at, :] = other.astype(BF16)
        return carry

    lax.fori_loop(0, 2 * tokens // step, one, 0)


def vmem_specs(n):
    return [pl.BlockSpec(memory_space=pltpu.VMEM)] * n


def call(kernel, outs, args, flops, scratch=(), specs=None):
    size = sum(a.size * a.dtype.itemsize for a in args)
    size += sum(o.size * o.dtype.itemsize for o in outs)
    return pl.pallas_call(
        kernel,
        out_shape=outs,
        in_specs=specs or vmem_specs(len(args)),
        out_specs=vmem_specs(len(outs)),
        scratch_shapes=list(scratch),
        compiler_params=pltpu.CompilerParams(vmem_limit_bytes=VMEM_LIMIT),
        cost_estimate=pl.CostEstimate(flops=flops, bytes_accessed=size, transcendentals=0),
    )(*args)


def shape(dims, dtype):
    return jax.ShapeDtypeStruct(dims, dtype)


def values_kernel(keep_ref, got_ref, k_ref, v_ref, total_ref, total16_ref):
    v = (keep_ref[...] + got_ref[...].astype(F32)).astype(BF16)
    v_ref[...] = v
    total = rows_by_rows(k_ref[...], v)
    total_ref[...] = total
    total16_ref[...] = total.astype(BF16)


def intra_kernel(blocks, q_ref, k_ref, v_ref, mixed_ref, local_ref):
    mask = causal_mask()
    state = jnp.zeros((DK, DK), F32)
    for i in range(blocks):
        q, k, v = (ref[block_rows(i), :] for ref in (q_ref, k_ref, v_ref))
        scores = jnp.where(mask, by_rows(q, k), 0.0).astype(BF16)
        earlier = state.astype(BF16)
        local_ref[i] = earlier
        mixed_ref[block_rows(i), :] = plain(scores, v) + plain(q, earlier)
        if i < blocks - 1:
            state = state + rows_by_rows(k, v)


def norm_kernel(mixed_ref, prior_ref, q_ref, up_ref, out_ref, gm_ref, total_ref, total16_ref):
    q = q_ref[...]
    mixed = mixed_ref[...] + plain(q, prior_ref[...].astype(BF16))
    inverse = lax.rsqrt(jnp.mean(mixed * mixed, axis=-1, keepdims=True) + norm_eps)
    normed = mixed * inverse
    out_ref[...] = normed.astype(BF16)
    up = up_ref[...].astype(F32)
    inner = jnp.mean(up * normed, axis=-1, keepdims=True)
    gm = ((up - normed * inner) * inverse).astype(BF16)
    gm_ref[...] = gm
    total = rows_by_rows(q, gm)
    total_ref[...] = total
    total16_ref[...] = total.astype(BF16)


def local_grad_kernel(
    blocks, q_ref, k_ref, v_ref, gm_ref, local_ref, prior_ref, gq_ref, gk_ref, gv_ref
):
    mask = causal_mask()
    state = jnp.zeros((DK, DK), F32)
    for i in reversed(range(blocks)):
        q, k, v, gm = (ref[block_rows(i), :] for ref in (q_ref, k_ref, v_ref, gm_ref))
        scores = jnp.where(mask, by_rows(q, k), 0.0).astype(BF16)
        gscores = jnp.where(mask, by_rows(gm, v), 0.0).astype(BF16)
        later = state.astype(BF16)
        prior = (prior_ref[...] + local_ref[i].astype(F32)).astype(BF16)
        gq_ref[block_rows(i), :] = (plain(gscores, k) + by_rows(gm, prior)).astype(BF16)
        gk_ref[block_rows(i), :] = rows_by_rows(gscores, q) + by_rows(v, later)
        gv_ref[block_rows(i), :] = rows_by_rows(scores, gm) + plain(k, later)
        if i:
            state = state + rows_by_rows(q, gm)


def grad_value_kernel(gv_ref, k_ref, after_ref, out_ref):
    out_ref[...] = (gv_ref[...] + plain(k_ref[...], after_ref[...].astype(BF16))).astype(BF16)


def grad_key_kernel(gk_ref, v_ref, after_ref, out_ref):
    out_ref[...] = (gk_ref[...] + by_rows(v_ref[...], after_ref[...].astype(BF16))).astype(BF16)


def latent_kernel(slabs, heads, *refs):
    own_ref, got_ref = refs[:2]
    piece_refs = refs[2 : 2 + 2 * heads]
    keep_ref, send_ref, x_ref, g_ref, sems = refs[2 + 2 * heads :]
    side, pair, head = place()
    tokens, width = piece_refs[0].shape
    copies = []
    for k in range(heads):
        for t in range(2):
            at = pl.multiple_of((side ^ t) * tokens, tokens)
            lane = pl.multiple_of((head ^ k) * width, width)
            copy = pltpu.make_async_copy(
                piece_refs[2 * k + t],
                x_ref.at[pl.ds(at, tokens), pl.ds(lane, width)],
                sems.at[2 * k + t],
            )
            copy.start()
            copies.append(copy)
    own, got = own_ref[...], got_ref[...]
    first = jnp.where(side == 0, own.astype(F32), got.astype(F32)).T.astype(BF16)
    second = jnp.where(side == 0, got.astype(F32), own.astype(F32)).T.astype(BF16)
    g_ref[:DK, :] = first
    g_ref[DK:, :] = second
    for copy in copies:
        copy.wait()
    rows = keep_ref.shape[-1]
    odd = lax.rem(pair, 2)
    for a in range(slabs):
        part = plain(g_ref[...], x_ref[:, a * rows : (a + 1) * rows])
        r = pair ^ a
        at = lax.div(r, 2)

        @pl.when(lax.rem(r, 2) == 0)
        def _():
            keep_ref[at] = part

        @pl.when(lax.rem(r, 2) == 1)
        def _():
            send_ref[at] = part.astype(BF16)


def sum_kernel(n, *refs):
    total = refs[0][...]
    for ref in refs[1:n]:
        total = total + ref[...].astype(F32)
    refs[n][...] = total.T


def pick(flag, even, odd):
    return jnp.where(flag == 0, even, odd)


def per_device(inputs, latent, queries, keys, grad_out):
    n, heads = lax.axis_size("seq"), lax.axis_size("head")
    side, pair, head = place()
    rows, columns = latent.shape
    tokens = inputs.shape[0]
    pairs, far = n // 2, n // 4
    blocks = 2 * tokens // BLOCK

    def half(flag):
        chunks = [
            pick(flag, inputs[:, 2 * c * rows :][:, :rows], inputs[:, (2 * c + 1) * rows :][:, :rows])
            for c in range(inputs.shape[1] // (2 * rows))
        ]
        return jnp.concatenate(chunks, axis=1)

    own_half = half(side)
    got_half = swap(half(1 - side), "seq", 1)
    pieces = [own_half, got_half]
    for k in range(1, heads):
        pieces += [swap(own_half, "head", k), swap(got_half, "head", k)]

    slab = latent.astype(BF16)
    sums = jnp.sum(jnp.abs(latent), axis=0)
    even = [slab] + [swap(slab, "seq", 4 * k) for k in range(1, far)]
    odd = [swap(a, "seq", 2) for a in even]
    slab_list = [a for two in zip(even, odd) for a in two]
    all_sums = lax.all_to_all(
        jnp.broadcast_to(sums[None], (n, columns)), "seq", 0, 0, tiled=True
    )

    def head_of(flag):
        return jnp.stack([pick(flag, a[:, :DK], a[:, DK:]) for a in (queries, keys, grad_out)])

    mine, theirs = head_of(side), swap(head_of(1 - side), "seq", 1)
    q, k, up = (
        jnp.concatenate([pick(side, mine[i], theirs[i]), pick(side, theirs[i], mine[i])], axis=0)
        for i in range(3)
    )

    any_specs = [pl.BlockSpec(memory_space=pl.ANY)] * len(pieces)
    keep, send = call(
        functools.partial(project_kernel, pairs, heads, n * rows),
        [shape((2 * tokens, DK), F32), shape((2 * tokens, DK), BF16)],
        slab_list + [all_sums] + pieces,
        2 * 2 * tokens * pairs * rows * columns,
        [
            pltpu.VMEM((2 * tokens, pairs * rows), BF16),
            pltpu.VMEM((pairs * rows, columns), BF16),
            pltpu.SemaphoreType.DMA((len(pieces),)),
        ],
        vmem_specs(pairs + 1) + any_specs,
    )
    long = 2 * tokens
    cost = 2 * long * DK * DK
    v, total, total16 = call(
        values_kernel,
        [shape((long, DK), BF16), shape((DK, DK), F32), shape((DK, DK), BF16)],
        [keep, swap(send, "seq", 1), k],
        cost,
    )

    def scan(total, total16, backward):
        before = jnp.zeros_like(total)
        distance = 1
        while distance < pairs:
            got = swap(total16, "seq", 2 * distance).astype(F32)
            high = lax.rem(lax.div(pair, distance), 2) == (0 if backward else 1)
            before = before + jnp.where(high, got, 0.0)
            total = total + got
            total16 = total.astype(BF16)
            distance *= 2
        return before

    prior = scan(total, total16, False)
    mixed, local = call(
        functools.partial(intra_kernel, blocks),
        [shape((long, DK), F32), shape((blocks, DK, DK), BF16)],
        [q, k, v],
        4 * cost,
    )
    out, gm, gtotal, gtotal16 = call(
        norm_kernel,
        [
            shape((long, DK), BF16),
            shape((long, DK), BF16),
            shape((DK, DK), F32),
            shape((DK, DK), BF16),
        ],
        [mixed, prior, q, up],
        2 * cost,
    )
    after = scan(gtotal, gtotal16, True)
    gq, gk_part, gv_part = call(
        functools.partial(local_grad_kernel, blocks),
        [shape((long, DK), BF16), shape((long, DK), F32), shape((long, DK), F32)],
        [q, k, v, gm, local, prior],
        9 * cost,
    )
    (gv,) = call(grad_value_kernel, [shape((long, DK), BF16)], [gv_part, k, after], cost)
    keep_parts, send_parts = call(
        functools.partial(latent_kernel, pairs, heads),
        [shape((far, columns, rows), F32), shape((far, columns, rows), BF16)],
        [gv, swap(gv, "seq", 1)] + pieces,
        2 * 2 * tokens * pairs * rows * columns,
        [
            pltpu.VMEM((2 * tokens, pairs * rows), BF16),
            pltpu.VMEM((columns, 2 * tokens), BF16),
            pltpu.SemaphoreType.DMA((len(pieces),)),
        ],
        vmem_specs(2) + any_specs,
    )
    (gk,) = call(grad_key_kernel, [shape((long, DK), BF16)], [gk_part, v, after], cost)

    arrived = []
    for i in reversed(range(1, far)):
        joined = keep_parts[i] + swap(send_parts[i], "seq", 2).astype(F32)
        arrived.append(swap(joined.astype(BF16), "seq", 4 * i))
    terms = [keep_parts[0], swap(send_parts[0], "seq", 2)] + arrived
    (grad_latent,) = call(
        functools.partial(sum_kernel, len(terms)), [shape((rows, columns), F32)], terms, 0
    )

    def token_half(flag):
        return jnp.stack([pick(flag, a[:tokens], a[tokens:]) for a in (out, gq, gk)])

    mine, theirs = token_half(side), swap(token_half(1 - side), "seq", 1)
    attn_out, grad_queries, grad_keys = (
        jnp.concatenate([pick(side, mine[i], theirs[i]), pick(side, theirs[i], mine[i])], axis=1)
        for i in range(3)
    )
    return (attn_out, grad_queries, grad_keys, grad_latent)


def solution(mesh):
    placed = (P("seq", "head"),) * 5
    return jax.shard_map(
        per_device,
        mesh=mesh,
        in_specs=placed,
        out_specs=(P("seq", "head"),) * 4,
        check_vma=False,
    )
```

time: 342 us -> 126 us (0.37)
  waiting for transfers between devices: 244 us -> 56.2 us
  starting transfers between devices: 0.2 us -> 33.2 us
  blocking collectives: 43.7 us -> 12.2 us
  matrix products: 14 us -> 0 us
  Pallas kernels: 0 us -> 13.9 us
  between operations: 14 us -> 0.98 us
  other arithmetic: 15.9 us -> 7.67 us
  local copies, waits for them, and re-layouts: 8.71 us -> 1.75 us
    all_gather x4 -> x0, waiting for transfers between devices: 157 us -> none  [the longest x2 123 us: entering(): gathered = lax.all_gather(array.astype(jnp.bfloat16), axis)]
    reduce_scatter x1 -> x0, waiting for transfers between devices: 86.4 us -> none  [per_device(): lax.psum_scatter(weight_term, 'seq', scatter_dimension=0, tiled=True)]
    ppermute x0 -> x27, waiting for transfers between devices: none -> 56.2 us  [swap(): return lax.ppermute(array, axis, [(i, i ^ distance) for i in range(count)])]
    psum x1 -> x0, blocking collectives: 43.7 us -> none  [per_device(): column_sums = lax.psum(jnp.sum(jnp.abs(latent), axis=0), 'seq')]
    ppermute x0 -> x27, starting transfers between devices: none -> 33.2 us  [swap(): return lax.ppermute(array, axis, [(i, i ^ distance) for i in range(count)])]
    dot_general x18 -> x0, matrix products: 14 us -> none  [the longest x1 5.44 us: per_device(): lax.dot_general(features_all, grad_flat, (((0,), (0,)), ((), ())), prefer...]
    pallas_call x0 -> x9, Pallas kernels: none -> 13.9 us  [call(): pl.pallas_call(kernel, out_shape=outs, in_specs=specs or vmem_specs(len(a...]
    all_to_all x0 -> x1, blocking collectives: none -> 12.2 us  [per_device(): lax.all_to_all(jnp.broadcast_to(sums[None], (n, columns)), 'seq', 0, 0, t...]
  transfers between devices with their start and end apart: 5 -> 27, of which waited for: 5 -> 15; matrix products, arithmetic and copies ran while one was open for 2% -> 2% of each run, Pallas kernels for 0% -> 9%
where the time goes in v1:
time: 126 us
  waiting for transfers between devices  56.2 us (45%)
  starting transfers between devices  33.2 us (26%)
  Pallas kernels  13.9 us (11%)
  blocking collectives  12.2 us (10%)
  other arithmetic  7.67 us (6%)
  local copies, waits for them, and re-layouts  1.75 us (1%)
    ppermute x27, waiting for transfers between devices, swap(): return lax.ppermute(array, axis, [(i, i ^ distance) for i in range(count)])  56.2 us
    ppermute x27, starting transfers between devices, swap(): return lax.ppermute(array, axis, [(i, i ^ distance) for i in range(count)])  33.2 us
    pallas_call x9, Pallas kernels, call(): pl.pallas_call(kernel, out_shape=outs, in_specs=specs or vmem_specs(len(a...  13.9 us
    all_to_all x1, blocking collectives, per_device(): lax.all_to_all(jnp.broadcast_to(sums[None], (n, columns)), 'seq', 0, 0, t...  12.2 us
  transfers between devices with their start and end apart: 27, of which 15 were waited for; matrix products, arithmetic and copies ran while one was open for 2% of the time, Pallas kernels for 9%

profile of v1, /device:TPU:0, one launch (start us, length us, event | category | flops | bytes accessed | tf_op | source)
XLA Modules:
  0.0 125.9 jit_solution(9307944183158465159)
XLA Ops:
  0.6 1.7 %broadcast_select_fusion.3 = (bf16[512,256]{1,0:T(8,128)(2,1)S(1)}, bf16[512,256]{1,0:T(8,128)(2,1)S(1)}, bf16[512,256]{1,0:T(8,128)(2,1)S(1)}, bf16[512,256]{1,...) fusion(pred[]{:T(512)S(6)} %eq.17, ...), kind=kLoop, calls=%fused_computation.21 | loop fusion | flops 1048576 | bytes 4194306 | tf_op jit(solution)/shard_map/jit(_where)/select_n | solution.py:228
  2.5 3.0 %collective-permute-start.8 = (bf16[512,1024]{1,0:T(8,128)(2,1)S(1)}, bf16[512,1024]{1,0:T(8,128)(2,1)S(1)}, u32[]{:S(2)}, u32[]{:S(2)}) collective-permute-start(bf16[512,1024]{1,0:T(8,128)(2,1)S(1)} %pad_maximum_fusion.1), channel_id=1, source_target_pairs={{0,2},{2,0},{4,6},{6,4},{8,10},{10,8},{12,14},{14,12},{16,18},{18,... | collective-permute-start | bytes 3145736 | tf_op jit(solution)/shard_map/ppermute | solution.py:50
  5.6 1.6 %collective-permute-start.1 = (bf16[256,256]{1,0:T(8,128)(2,1)S(1)}, bf16[256,256]{1,0:T(8,128)(2,1)S(1)}, u32[]{:S(2)}, u32[]{:S(2)}) collective-permute-start(bf16[256,256]{1,0:T(8,128)(2,1)S(1)} %get-tuple-element.72.refs_0_), channel_id=1, source_target_pairs={{0,4},{2,6},{4,0},{6,2},{8,12},{10,14},{12,8},{14,10},{16,20},{18,... | collective-permute-start | bytes 393224 | tf_op jit(solution)/shard_map/ppermute | solution.py:50
  7.1 1.6 %collective-permute-start.2 = (bf16[256,256]{1,0:T(8,128)(2,1)S(1)}, bf16[256,256]{1,0:T(8,128)(2,1)S(1)}, u32[]{:S(2)}, u32[]{:S(2)}) collective-permute-start(bf16[256,256]{1,0:T(8,128)(2,1)S(1)} %get-tuple-element.72.refs_0_), channel_id=1, source_target_pairs={{0,8},{2,10},{4,12},{6,14},{8,0},{10,2},{12,4},{14,6},{16,24},{18,... | collective-permute-start | bytes 393224 | tf_op jit(solution)/shard_map/ppermute | solution.py:50
  8.7 2.6 %collective-permute-start.4 = (bf16[256,256]{1,0:T(8,128)(2,1)S(1)}, bf16[256,256]{1,0:T(8,128)(2,1)S(1)}, u32[]{:S(2)}, u32[]{:S(2)}) collective-permute-start(bf16[256,256]{1,0:T(8,128)(2,1)S(1)} %get-tuple-element.72.refs_0_), channel_id=1, source_target_pairs={{0,16},{2,18},{4,20},{6,22},{8,24},{10,26},{12,28},{14,30},{16,0},... | collective-permute-start | bytes 393224 | tf_op jit(solution)/shard_map/ppermute | solution.py:50
  11.5 17.1 %collective-permute-done.8.refs_10_.refs_3_ = bf16[512,1024]{1,0:T(8,128)(2,1)S(1)} collective-permute-done((bf16[512,1024]{1,0:T(8,128)(2,1)S(1)}, bf16[512,1024]{1,0:T(8,128)(2,1)S(1)}, u32[]{:S(2)}, u32[]{:S(2)}) %collective-permute-start.8) | collective-permute-done | bytes 1048608 | tf_op jit(solution)/shard_map/ppermute | solution.py:50
  28.8 1.8 %collective-permute-start = (bf16[3,512,128]{2,1,0:T(8,128)(2,1)S(1)}, bf16[3,512,128]{2,1,0:T(8,128)(2,1)S(1)}, u32[]{:S(2)}, u32[]{:S(2)}) collective-permute-start(bf16[3,512,128]{2,1,0:T(8,128)(2,1)S(1)} %pad_maximum_fusion.2), channel_id=1, source_target_pairs={{0,2},{2,0},{4,6},{6,4},{8,10},{10,8},{12,14},{14,12},{16,18},{18,... | collective-permute-start | bytes 1179656 | tf_op jit(solution)/shard_map/ppermute | solution.py:50
  30.6 3.6 %collective-permute-start.6 = (bf16[256,256]{1,0:T(8,128)(2,1)S(1)}, bf16[256,256]{1,0:T(8,128)(2,1)S(1)}, u32[]{:S(2)}, u32[]{:S(2)}) collective-permute-start(bf16[256,256]{1,0:T(8,128)(2,1)S(1)} %get-tuple-element.72.refs_0_), channel_id=1, source_target_pairs={{0,24},{2,26},{4,28},{6,30},{8,16},{10,18},{12,20},{14,22},{16,8},... | collective-permute-start | bytes 393224 | tf_op jit(solution)/shard_map/ppermute | solution.py:50
  34.2 1.5 %collective-permute-start.3 = (bf16[256,256]{1,0:T(8,128)(2,1)S(1)}, bf16[256,256]{1,0:T(8,128)(2,1)S(1)}, u32[]{:S(2)}, u32[]{:S(2)}) collective-permute-start(bf16[256,256]{1,0:T(8,128)(2,1)S(1)} %collective-permute-done.2.refs_2_), channel_id=1, source_target_pairs={{0,4},{2,6},{4,0},{6,2},{8,12},{10,14},{12,8},{14,10},{16,20},{18,... | collective-permute-start | bytes 393224 | tf_op jit(solution)/shard_map/ppermute | solution.py:50
  35.8 2.5 %collective-permute-done.6.refs_6_ = bf16[256,256]{1,0:T(8,128)(2,1)S(1)} collective-permute-done((bf16[256,256]{1,0:T(8,128)(2,1)S(1)}, bf16[256,256]{1,0:T(8,128)(2,1)S(1)}, u32[]{:S(2)}, u32[]{:S(2)}) %collective-permute-start.6) | collective-permute-done | bytes 131104 | tf_op jit(solution)/shard_map/ppermute | solution.py:50
  38.2 1.5 %collective-permute-start.5 = (bf16[256,256]{1,0:T(8,128)(2,1)S(1)}, bf16[256,256]{1,0:T(8,128)(2,1)S(1)}, u32[]{:S(2)}, u32[]{:S(2)}) collective-permute-start(bf16[256,256]{1,0:T(8,128)(2,1)S(1)} %collective-permute-done.4.refs_4_), channel_id=1, source_target_pairs={{0,4},{2,6},{4,0},{6,2},{8,12},{10,14},{12,8},{14,10},{16,20},{18,... | collective-permute-start | bytes 393224 | tf_op jit(solution)/shard_map/ppermute | solution.py:50
  41.1 12.2 %all_to_all.8 = f32[16,1,256]{2,1,0:T(1,128)S(1)} all-to-all(f32[16,1,256]{2,1,0:T(1,128)S(1)} %broadcast_in_dim.15), channel_id=1, replica_groups=mesh['seq'=16,'head'=2] {'seq'}, dimensions={0} | all-to-all | bytes 32768 | tf_op jit(solution)/shard_map/all_to_all | solution.py:257
  53.3 3.0 %shard_map.84 = (f32[1024,128]{1,0:T(8,128)S(1)}, bf16[1024,128]{1,0:T(8,128)(2,1)S(1)}) custom-call(bf16[256,256]{1,0:T(8,128)(2,1)S(1)} %get-tuple-element.72.refs_0_, bf16[256,256]{1,0:T(8,128)(2,1)S(1)} %collective-permute-done.1.refs_1_, bf16[256,256]{1,0:T(8,128)(2,1)S(1)} %collective-permute-done.2.refs_2_, ...), custom_call_target="tpu_custom_call" | custom-call | flops 1073741824 | bytes 6045696 | tf_op jit(solution)/shard_map/pallas_call | solution.py:102
  57.1 5.6 %collective-permute-done.11.got_ref = bf16[1024,128]{1,0:T(8,128)(2,1)S(1)} collective-permute-done((bf16[1024,128]{1,0:T(8,128)(2,1)S(1)}, bf16[1024,128]{1,0:T(8,128)(2,1)S(1)}, u32[]{:S(2)}, u32[]{:S(2)}) %collective-permute-start.11) | collective-permute-done | bytes 262176 | tf_op jit(solution)/shard_map/ppermute | solution.py:50
  63.7 3.3 %collective-permute-done.12 = bf16[128,128]{1,0:T(8,128)(2,1)S(1)} collective-permute-done((bf16[128,128]{1,0:T(8,128)(2,1)S(1)}, bf16[128,128]{1,0:T(8,128)(2,1)S(1)}, u32[]{:S(2)}, u32[]{:S(2)}) %collective-permute-start.12) | collective-permute-done | bytes 32800 | tf_op jit(solution)/shard_map/ppermute | solution.py:50
  67.7 3.3 %collective-permute-done.13 = bf16[128,128]{1,0:T(8,128)(2,1)S(1)} collective-permute-done((bf16[128,128]{1,0:T(8,128)(2,1)S(1)}, bf16[128,128]{1,0:T(8,128)(2,1)S(1)}, u32[]{:S(2)}, u32[]{:S(2)}) %collective-permute-start.13) | collective-permute-done | bytes 32800 | tf_op jit(solution)/shard_map/ppermute | solution.py:50
  71.7 1.4 %shard_map.86 = (f32[1024,128]{1,0:T(8,128)S(1)}, bf16[8,128,128]{2,1,0:T(8,128)(2,1)S(1)}) custom-call(bf16[1024,128]{1,0:T(8,128)(2,1)S(1)} %pad_maximum_fusion.4.q_ref, bf16[1024,128]{1,0:T(8,128)(2,1)S(1)} %pad_maximum_fusion.5.k_ref, bf16[1024,128]{1,0:T(8,128)(2,1)S(1)} %get-tuple-element.22.v_ref), custom_call_target="tpu_custom_call" | custom-call | flops 134217728 | bytes 1572864 | tf_op jit(solution)/shard_map/pallas_call | solution.py:102
  73.2 3.1 %collective-permute-done.14 = bf16[128,128]{1,0:T(8,128)(2,1)S(1)} collective-permute-done((bf16[128,128]{1,0:T(8,128)(2,1)S(1)}, bf16[128,128]{1,0:T(8,128)(2,1)S(1)}, u32[]{:S(2)}, u32[]{:S(2)}) %collective-permute-start.14) | collective-permute-done | bytes 32800 | tf_op jit(solution)/shard_map/ppermute | solution.py:50
  78.3 3.4 %collective-permute-done.15 = bf16[128,128]{1,0:T(8,128)(2,1)} collective-permute-done((bf16[128,128]{1,0:T(8,128)(2,1)S(1)}, bf16[128,128]{1,0:T(8,128)(2,1)}, u32[]{:S(2)}, u32[]{:S(2)}) %collective-permute-start.15) | collective-permute-done | bytes 32800 | tf_op jit(solution)/shard_map/ppermute | solution.py:50
  83.5 3.9 %collective-permute-done.16 = bf16[128,128]{1,0:T(8,128)(2,1)} collective-permute-done((bf16[128,128]{1,0:T(8,128)(2,1)}, bf16[128,128]{1,0:T(8,128)(2,1)}, u32[]{:S(2)}, u32[]{:S(2)}) %collective-permute-start.16) | collective-permute-done | bytes 32800 | tf_op jit(solution)/shard_map/ppermute | solution.py:50
  89.5 1.9 %shard_map.88 = (bf16[1024,128]{1,0:T(8,128)(2,1)S(1)}, f32[1024,128]{1,0:T(8,128)S(1)}, f32[1024,128]{1,0:T(8,128)S(1)}) custom-call(bf16[1024,128]{1,0:T(8,128)(2,1)S(1)} %pad_maximum_fusion.4.q_ref, bf16[1024,128]{1,0:T(8,128)(2,1)S(1)} %pad_maximum_fusion.5.k_ref, bf16[1024,128]{1,0:T(8,128)(2,1)S(1)} %get-tuple-element.22.v_ref, ...), custom_call_target="tpu_custom_call" | custom-call | flops 301989888 | bytes 2686976 | tf_op jit(solution)/shard_map/pallas_call | solution.py:102
  91.4 1.8 %collective-permute-done.17 = bf16[128,128]{1,0:T(8,128)(2,1)S(1)} collective-permute-done((bf16[128,128]{1,0:T(8,128)(2,1)S(1)}, bf16[128,128]{1,0:T(8,128)(2,1)S(1)}, u32[]{:S(2)}, u32[]{:S(2)}) %collective-permute-start.17) | collective-permute-done | bytes 32800 | tf_op jit(solution)/shard_map/ppermute | solution.py:50
  95.1 1.6 %collective-permute-start.18 = (bf16[3,512,128]{2,1,0:T(8,128)(2,1)S(1)}, bf16[3,512,128]{2,1,0:T(8,128)(2,1)S(1)}, u32[]{:S(2)}, u32[]{:S(2)}) collective-permute-start(bf16[3,512,128]{2,1,0:T(8,128)(2,1)S(1)} %pad_maximum_fusion.3), channel_id=1, source_target_pairs={{0,2},{2,0},{4,6},{6,4},{8,10},{10,8},{12,14},{14,12},{16,18},{18,... | collective-permute-start | bytes 1179656 | tf_op jit(solution)/shard_map/ppermute | solution.py:50
  96.7 4.2 %collective-permute-done.19.refs_1_ = bf16[1024,128]{1,0:T(8,128)(2,1)S(1)} collective-permute-done((bf16[1024,128]{1,0:T(8,128)(2,1)S(1)}, bf16[1024,128]{1,0:T(8,128)(2,1)S(1)}, u32[]{:S(2)}, u32[]{:S(2)}) %collective-permute-start.19) | collective-permute-done | bytes 262176 | tf_op jit(solution)/shard_map/ppermute | solution.py:50
  100.9 5.3 %shard_map.91 = (f32[4,256,256]{2,1,0:T(8,128)S(1)}, bf16[4,256,256]{2,1,0:T(8,128)(2,1)S(1)}) custom-call(bf16[1024,128]{1,0:T(8,128)(2,1)S(1)} %shard_map.90.refs_0_, bf16[1024,128]{1,0:T(8,128)(2,1)S(1)} %collective-permute-done.19.refs_1_, bf16[512,1024]{1,0:T(8,128)(2,1)S(1)} %pad_maximum_fusion.refs_9_.refs_2_, ...), custom_call_target="tpu_custom_call" | custom-call | flops 1073741824 | bytes 6291456 | tf_op jit(solution)/shard_map/pallas_call | solution.py:102
  106.9 1.4 %collective-permute-start.25 = (bf16[256,256]{1,0:T(8,128)(2,1)S(1)}, bf16[256,256]{1,0:T(8,128)(2,1)S(1)}, u32[]{:S(2)}, u32[]{:S(2)}) collective-permute-start(bf16[256,256]{1,0:T(8,128)(2,1)S(1)} %get-tuple-element.59), channel_id=1, source_target_pairs={{0,4},{2,6},{4,0},{6,2},{8,12},{10,14},{12,8},{14,10},{16,20},{18,... | collective-permute-start | bytes 393224 | tf_op jit(solution)/shard_map/ppermute | solution.py:50
  108.9 1.4 %collective-permute-start.21 = (bf16[256,256]{1,0:T(8,128)(2,1)S(1)}, bf16[256,256]{1,0:T(8,128)(2,1)S(1)}, u32[]{:S(2)}, u32[]{:S(2)}) collective-permute-start(bf16[256,256]{1,0:T(8,128)(2,1)S(1)} %get-tuple-element.61), channel_id=1, source_target_pairs={{0,4},{2,6},{4,0},{6,2},{8,12},{10,14},{12,8},{14,10},{16,20},{18,... | collective-permute-start | bytes 393224 | tf_op jit(solution)/shard_map/ppermute | solution.py:50
  110.3 2.3 %collective-permute-done.25 = bf16[256,256]{1,0:T(8,128)(2,1)S(1)} collective-permute-done((bf16[256,256]{1,0:T(8,128)(2,1)S(1)}, bf16[256,256]{1,0:T(8,128)(2,1)S(1)}, u32[]{:S(2)}, u32[]{:S(2)}) %collective-permute-start.25) | collective-permute-done | bytes 131104 | tf_op jit(solution)/shard_map/ppermute | solution.py:50
  112.6 1.4 %collective-permute-done.23 = bf16[256,256]{1,0:T(8,128)(2,1)S(1)} collective-permute-done((bf16[256,256]{1,0:T(8,128)(2,1)S(1)}, bf16[256,256]{1,0:T(8,128)(2,1)S(1)}, u32[]{:S(2)}, u32[]{:S(2)}) %collective-permute-start.23) | collective-permute-done | bytes 131104 | tf_op jit(solution)/shard_map/ppermute | solution.py:50
  114.0 1.4 %collective-permute-done.21 = bf16[256,256]{1,0:T(8,128)(2,1)S(1)} collective-permute-done((bf16[256,256]{1,0:T(8,128)(2,1)S(1)}, bf16[256,256]{1,0:T(8,128)(2,1)S(1)}, u32[]{:S(2)}, u32[]{:S(2)}) %collective-permute-start.21) | collective-permute-done | bytes 131104 | tf_op jit(solution)/shard_map/ppermute | solution.py:50
  117.3 2.7 %collective-permute-start.26 = (bf16[256,256]{1,0:T(8,128)(2,1)S(1)}, bf16[256,256]{1,0:T(8,128)(2,1)S(1)}, u32[]{:S(2)}, u32[]{:S(2)}) collective-permute-start(bf16[256,256]{1,0:T(8,128)(2,1)S(1)} %get-tuple-element.44), channel_id=1, source_target_pairs={{0,8},{2,10},{4,12},{6,14},{8,0},{10,2},{12,4},{14,6},{16,24},{18,... | collective-permute-start | bytes 393224 | tf_op jit(solution)/shard_map/ppermute | solution.py:50
  122.6 2.5 %collective-permute-done.24.refs_3_ = bf16[256,256]{1,0:T(8,128)(2,1)S(1)} collective-permute-done((bf16[256,256]{1,0:T(8,128)(2,1)S(1)}, bf16[256,256]{1,0:T(8,128)(2,1)S(1)}, u32[]{:S(2)}, u32[]{:S(2)}) %collective-permute-start.24) | collective-permute-done | bytes 131104 | tf_op jit(solution)/shard_map/ppermute | solution.py:50
  (80 shorter events, 19.2 us)
Async XLA Ops:
  2.3 3.2 %copy-start.8 = (f32[256,256]{1,0:T(8,128)S(1)}, f32[256,256]{1,0:T(8,128)}, u32[]{:S(2)}) copy-start(f32[256,256]{1,0:T(8,128)} %param.6) | copy-start | bytes 786436
  2.3 26.3 %copy-start.5 = (bf16[512,256]{1,0:T(8,128)(2,1)S(1)}, bf16[512,256]{1,0:T(8,128)(2,1)}, u32[]{:S(2)}) copy-start(bf16[512,256]{1,0:T(8,128)(2,1)} %param.9) | copy-start | bytes 786436
  2.3 26.4 %copy-start.6 = (bf16[512,256]{1,0:T(8,128)(2,1)S(1)}, bf16[512,256]{1,0:T(8,128)(2,1)}, u32[]{:S(2)}) copy-start(bf16[512,256]{1,0:T(8,128)(2,1)} %param.8) | copy-start | bytes 786436
  2.5 26.2 %copy-start.7 = (bf16[512,256]{1,0:T(8,128)(2,1)S(1)}, bf16[512,256]{1,0:T(8,128)(2,1)}, u32[]{:S(2)}) copy-start(bf16[512,256]{1,0:T(8,128)(2,1)} %param.7) | copy-start | bytes 786436
  2.5 26.2 %collective-permute-start.8 = (bf16[512,1024]{1,0:T(8,128)(2,1)S(1)}, bf16[512,1024]{1,0:T(8,128)(2,1)S(1)}, u32[]{:S(2)}, u32[]{:S(2)}) collective-permute-start(bf16[512,1024]{1,0:T(8,128)(2,1)S(1)} %pad_maximum_fusion.1), channel_id=1, source_target_pairs={{0,2},{2,0},{4,6},{6,4},{8,10},{10,8},{12,14},{14,12},{16,18},{18,... | collective-permute-start | bytes 3145736 | tf_op jit(solution)/shard_map/ppermute | solution.py:50
  5.6 23.3 %collective-permute-start.1 = (bf16[256,256]{1,0:T(8,128)(2,1)S(1)}, bf16[256,256]{1,0:T(8,128)(2,1)S(1)}, u32[]{:S(2)}, u32[]{:S(2)}) collective-permute-start(bf16[256,256]{1,0:T(8,128)(2,1)S(1)} %get-tuple-element.72.refs_0_), channel_id=1, source_target_pairs={{0,4},{2,6},{4,0},{6,2},{8,12},{10,14},{12,8},{14,10},{16,20},{18,... | collective-permute-start | bytes 393224 | tf_op jit(solution)/shard_map/ppermute | solution.py:50
  7.1 23.5 %collective-permute-start.2 = (bf16[256,256]{1,0:T(8,128)(2,1)S(1)}, bf16[256,256]{1,0:T(8,128)(2,1)S(1)}, u32[]{:S(2)}, u32[]{:S(2)}) collective-permute-start(bf16[256,256]{1,0:T(8,128)(2,1)S(1)} %get-tuple-element.72.refs_0_), channel_id=1, source_target_pairs={{0,8},{2,10},{4,12},{6,14},{8,0},{10,2},{12,4},{14,6},{16,24},{18,... | collective-permute-start | bytes 393224 | tf_op jit(solution)/shard_map/ppermute | solution.py:50
  8.7 25.5 %collective-permute-start.4 = (bf16[256,256]{1,0:T(8,128)(2,1)S(1)}, bf16[256,256]{1,0:T(8,128)(2,1)S(1)}, u32[]{:S(2)}, u32[]{:S(2)}) collective-permute-start(bf16[256,256]{1,0:T(8,128)(2,1)S(1)} %get-tuple-element.72.refs_0_), channel_id=1, source_target_pairs={{0,16},{2,18},{4,20},{6,22},{8,24},{10,26},{12,28},{14,30},{16,0},... | collective-permute-start | bytes 393224 | tf_op jit(solution)/shard_map/ppermute | solution.py:50
  11.4 41.9 %collective-permute-start.9 = (bf16[512,1024]{1,0:T(8,128)(2,1)S(1)}, bf16[512,1024]{1,0:T(8,128)(2,1)S(1)}, u32[]{:S(2)}, u32[]{:S(2)}) collective-permute-start(bf16[512,1024]{1,0:T(8,128)(2,1)S(1)} %pad_maximum_fusion.refs_9_.refs_2_), channel_id=1, source_target_pairs={{0,1},{1,0},{2,3},{3,2},{4,5},{5,4},{6,7},{7,6},{8,9},{9,8},{10,11... | collective-permute-start | bytes 3145736 | tf_op jit(solution)/shard_map/ppermute | solution.py:50
  28.7 24.7 %collective-permute-start.10 = (bf16[512,1024]{1,0:T(8,128)(2,1)S(1)}, bf16[512,1024]{1,0:T(8,128)(2,1)S(1)}, u32[]{:S(2)}, u32[]{:S(2)}) collective-permute-start(bf16[512,1024]{1,0:T(8,128)(2,1)S(1)} %collective-permute-done.8.refs_10_.refs_3_), channel_id=1, source_target_pairs={{0,1},{1,0},{2,3},{3,2},{4,5},{5,4},{6,7},{7,6},{8,9},{9,8},{10,11... | collective-permute-start | bytes 3145736 | tf_op jit(solution)/shard_map/ppermute | solution.py:50
  28.8 28.2 %collective-permute-start = (bf16[3,512,128]{2,1,0:T(8,128)(2,1)S(1)}, bf16[3,512,128]{2,1,0:T(8,128)(2,1)S(1)}, u32[]{:S(2)}, u32[]{:S(2)}) collective-permute-start(bf16[3,512,128]{2,1,0:T(8,128)(2,1)S(1)} %pad_maximum_fusion.2), channel_id=1, source_target_pairs={{0,2},{2,0},{4,6},{6,4},{8,10},{10,8},{12,14},{14,12},{16,18},{18,... | collective-permute-start | bytes 1179656 | tf_op jit(solution)/shard_map/ppermute | solution.py:50
  30.6 7.6 %collective-permute-start.6 = (bf16[256,256]{1,0:T(8,128)(2,1)S(1)}, bf16[256,256]{1,0:T(8,128)(2,1)S(1)}, u32[]{:S(2)}, u32[]{:S(2)}) collective-permute-start(bf16[256,256]{1,0:T(8,128)(2,1)S(1)} %get-tuple-element.72.refs_0_), channel_id=1, source_target_pairs={{0,24},{2,26},{4,28},{6,30},{8,16},{10,18},{12,20},{14,22},{16,8},... | collective-permute-start | bytes 393224 | tf_op jit(solution)/shard_map/ppermute | solution.py:50
  34.2 5.5 %collective-permute-start.3 = (bf16[256,256]{1,0:T(8,128)(2,1)S(1)}, bf16[256,256]{1,0:T(8,128)(2,1)S(1)}, u32[]{:S(2)}, u32[]{:S(2)}) collective-permute-start(bf16[256,256]{1,0:T(8,128)(2,1)S(1)} %collective-permute-done.2.refs_2_), channel_id=1, source_target_pairs={{0,4},{2,6},{4,0},{6,2},{8,12},{10,14},{12,8},{14,10},{16,20},{18,... | collective-permute-start | bytes 393224 | tf_op jit(solution)/shard_map/ppermute | solution.py:50
  38.2 15.1 %collective-permute-start.5 = (bf16[256,256]{1,0:T(8,128)(2,1)S(1)}, bf16[256,256]{1,0:T(8,128)(2,1)S(1)}, u32[]{:S(2)}, u32[]{:S(2)}) collective-permute-start(bf16[256,256]{1,0:T(8,128)(2,1)S(1)} %collective-permute-done.4.refs_4_), channel_id=1, source_target_pairs={{0,4},{2,6},{4,0},{6,2},{8,12},{10,14},{12,8},{14,10},{16,20},{18,... | collective-permute-start | bytes 393224 | tf_op jit(solution)/shard_map/ppermute | solution.py:50
  39.8 13.5 %collective-permute-start.7 = (bf16[256,256]{1,0:T(8,128)(2,1)S(1)}, bf16[256,256]{1,0:T(8,128)(2,1)S(1)}, u32[]{:S(2)}, u32[]{:S(2)}) collective-permute-start(bf16[256,256]{1,0:T(8,128)(2,1)S(1)} %collective-permute-done.6.refs_6_), channel_id=1, source_target_pairs={{0,4},{2,6},{4,0},{6,2},{8,12},{10,14},{12,8},{14,10},{16,20},{18,... | collective-permute-start | bytes 393224 | tf_op jit(solution)/shard_map/ppermute | solution.py:50
  56.3 6.4 %collective-permute-start.11 = (bf16[1024,128]{1,0:T(8,128)(2,1)S(1)}, bf16[1024,128]{1,0:T(8,128)(2,1)S(1)}, u32[]{:S(2)}, u32[]{:S(2)}) collective-permute-start(bf16[1024,128]{1,0:T(8,128)(2,1)S(1)} %get-tuple-element.21), channel_id=1, source_target_pairs={{0,2},{2,0},{4,6},{6,4},{8,10},{10,8},{12,14},{14,12},{16,18},{18,... | collective-permute-start | bytes 786440 | tf_op jit(solution)/shard_map/ppermute | solution.py:50
  63.1 4.0 %collective-permute-start.12 = (bf16[128,128]{1,0:T(8,128)(2,1)S(1)}, bf16[128,128]{1,0:T(8,128)(2,1)S(1)}, u32[]{:S(2)}, u32[]{:S(2)}) collective-permute-start(bf16[128,128]{1,0:T(8,128)(2,1)S(1)} %get-tuple-element.24), channel_id=1, source_target_pairs={{0,4},{2,6},{4,0},{6,2},{8,12},{10,14},{12,8},{14,10},{16,20},{18,... | collective-permute-start | bytes 98312 | tf_op jit(solution)/shard_map/ppermute | solution.py:50
  67.1 4.0 %collective-permute-start.13 = (bf16[128,128]{1,0:T(8,128)(2,1)S(1)}, bf16[128,128]{1,0:T(8,128)(2,1)S(1)}, u32[]{:S(2)}, u32[]{:S(2)}) collective-permute-start(bf16[128,128]{1,0:T(8,128)(2,1)S(1)} %fusion.9), channel_id=1, source_target_pairs={{0,8},{2,10},{4,12},{6,14},{8,0},{10,2},{12,4},{14,6},{16,24},{18,... | collective-permute-start | bytes 98312 | tf_op jit(solution)/shard_map/ppermute | solution.py:50
  71.1 5.2 %collective-permute-start.14 = (bf16[128,128]{1,0:T(8,128)(2,1)S(1)}, bf16[128,128]{1,0:T(8,128)(2,1)S(1)}, u32[]{:S(2)}, u32[]{:S(2)}) collective-permute-start(bf16[128,128]{1,0:T(8,128)(2,1)S(1)} %fusion.5), channel_id=1, source_target_pairs={{0,16},{2,18},{4,20},{6,22},{8,24},{10,26},{12,28},{14,30},{16,0},... | collective-permute-start | bytes 98312 | tf_op jit(solution)/shard_map/ppermute | solution.py:50
  77.7 4.0 %collective-permute-start.15 = (bf16[128,128]{1,0:T(8,128)(2,1)S(1)}, bf16[128,128]{1,0:T(8,128)(2,1)}, u32[]{:S(2)}, u32[]{:S(2)}) collective-permute-start(bf16[128,128]{1,0:T(8,128)(2,1)S(1)} %get-tuple-element.31), channel_id=1, source_target_pairs={{0,4},{2,6},{4,0},{6,2},{8,12},{10,14},{12,8},{14,10},{16,20},{18,... | collective-permute-start | bytes 98312 | tf_op jit(solution)/shard_map/ppermute | solution.py:50
  83.1 4.2 %collective-permute-start.16 = (bf16[128,128]{1,0:T(8,128)(2,1)}, bf16[128,128]{1,0:T(8,128)(2,1)}, u32[]{:S(2)}, u32[]{:S(2)}) collective-permute-start(bf16[128,128]{1,0:T(8,128)(2,1)} %fusion.10), channel_id=1, source_target_pairs={{0,8},{2,10},{4,12},{6,14},{8,0},{10,2},{12,4},{14,6},{16,24},{18,... | collective-permute-start | bytes 98312 | tf_op jit(solution)/shard_map/ppermute | solution.py:50
  88.2 5.0 %collective-permute-start.17 = (bf16[128,128]{1,0:T(8,128)(2,1)S(1)}, bf16[128,128]{1,0:T(8,128)(2,1)S(1)}, u32[]{:S(2)}, u32[]{:S(2)}) collective-permute-start(bf16[128,128]{1,0:T(8,128)(2,1)S(1)} %fusion.8), channel_id=1, source_target_pairs={{0,16},{2,18},{4,20},{6,22},{8,24},{10,26},{12,28},{14,30},{16,0},... | collective-permute-start | bytes 98312 | tf_op jit(solution)/shard_map/ppermute | solution.py:50
  91.4 9.5 %copy-start.1 = (bf16[512,1024]{1,0:T(8,128)(2,1)S(1)}, bf16[512,1024]{1,0:T(8,128)(2,1)}, u32[]{:S(2)}) copy-start(bf16[512,1024]{1,0:T(8,128)(2,1)} %copy-done) | copy-start | bytes 3145732
  94.4 6.4 %collective-permute-start.19 = (bf16[1024,128]{1,0:T(8,128)(2,1)S(1)}, bf16[1024,128]{1,0:T(8,128)(2,1)S(1)}, u32[]{:S(2)}, u32[]{:S(2)}) collective-permute-start(bf16[1024,128]{1,0:T(8,128)(2,1)S(1)} %shard_map.90.refs_0_), channel_id=1, source_target_pairs={{0,2},{2,0},{4,6},{6,4},{8,10},{10,8},{12,14},{14,12},{16,18},{18,... | collective-permute-start | bytes 786440 | tf_op jit(solution)/shard_map/ppermute | solution.py:50
  95.1 24.9 %collective-permute-start.18 = (bf16[3,512,128]{2,1,0:T(8,128)(2,1)S(1)}, bf16[3,512,128]{2,1,0:T(8,128)(2,1)S(1)}, u32[]{:S(2)}, u32[]{:S(2)}) collective-permute-start(bf16[3,512,128]{2,1,0:T(8,128)(2,1)S(1)} %pad_maximum_fusion.3), channel_id=1, source_target_pairs={{0,2},{2,0},{4,6},{6,4},{8,10},{10,8},{12,14},{14,12},{16,18},{18,... | collective-permute-start | bytes 1179656 | tf_op jit(solution)/shard_map/ppermute | solution.py:50
  106.2 16.1 %collective-permute-start.20 = (bf16[256,256]{1,0:T(8,128)(2,1)S(1)}, bf16[256,256]{1,0:T(8,128)(2,1)S(1)}, u32[]{:S(2)}, u32[]{:S(2)}) collective-permute-start(bf16[256,256]{1,0:T(8,128)(2,1)S(1)} %get-tuple-element.62), channel_id=1, source_target_pairs={{0,4},{2,6},{4,0},{6,2},{8,12},{10,14},{12,8},{14,10},{16,20},{18,... | collective-permute-start | bytes 393224 | tf_op jit(solution)/shard_map/ppermute | solution.py:50
  106.9 5.8 %collective-permute-start.25 = (bf16[256,256]{1,0:T(8,128)(2,1)S(1)}, bf16[256,256]{1,0:T(8,128)(2,1)S(1)}, u32[]{:S(2)}, u32[]{:S(2)}) collective-permute-start(bf16[256,256]{1,0:T(8,128)(2,1)S(1)} %get-tuple-element.59), channel_id=1, source_target_pairs={{0,4},{2,6},{4,0},{6,2},{8,12},{10,14},{12,8},{14,10},{16,20},{18,... | collective-permute-start | bytes 393224 | tf_op jit(solution)/shard_map/ppermute | solution.py:50
  108.3 5.8 %collective-permute-start.23 = (bf16[256,256]{1,0:T(8,128)(2,1)S(1)}, bf16[256,256]{1,0:T(8,128)(2,1)S(1)}, u32[]{:S(2)}, u32[]{:S(2)}) collective-permute-start(bf16[256,256]{1,0:T(8,128)(2,1)S(1)} %get-tuple-element.60), channel_id=1, source_target_pairs={{0,4},{2,6},{4,0},{6,2},{8,12},{10,14},{12,8},{14,10},{16,20},{18,... | collective-permute-start | bytes 393224 | tf_op jit(solution)/shard_map/ppermute | solution.py:50
  108.9 6.6 %collective-permute-start.21 = (bf16[256,256]{1,0:T(8,128)(2,1)S(1)}, bf16[256,256]{1,0:T(8,128)(2,1)S(1)}, u32[]{:S(2)}, u32[]{:S(2)}) collective-permute-start(bf16[256,256]{1,0:T(8,128)(2,1)S(1)} %get-tuple-element.61), channel_id=1, source_target_pairs={{0,4},{2,6},{4,0},{6,2},{8,12},{10,14},{12,8},{14,10},{16,20},{18,... | collective-permute-start | bytes 393224 | tf_op jit(solution)/shard_map/ppermute | solution.py:50
  115.5 7.0 %collective-permute-start.22 = (bf16[256,256]{1,0:T(8,128)(2,1)S(1)}, bf16[256,256]{1,0:T(8,128)(2,1)S(1)}, u32[]{:S(2)}, u32[]{:S(2)}) collective-permute-start(bf16[256,256]{1,0:T(8,128)(2,1)S(1)} %get-tuple-element.46), channel_id=1, source_target_pairs={{0,24},{2,26},{4,28},{6,30},{8,16},{10,18},{12,20},{14,22},{16,8},... | collective-permute-start | bytes 393224 | tf_op jit(solution)/shard_map/ppermute | solution.py:50
  116.4 8.7 %collective-permute-start.24 = (bf16[256,256]{1,0:T(8,128)(2,1)S(1)}, bf16[256,256]{1,0:T(8,128)(2,1)S(1)}, u32[]{:S(2)}, u32[]{:S(2)}) collective-permute-start(bf16[256,256]{1,0:T(8,128)(2,1)S(1)} %get-tuple-element.45), channel_id=1, source_target_pairs={{0,16},{2,18},{4,20},{6,22},{8,24},{10,26},{12,28},{14,30},{16,0},... | collective-permute-start | bytes 393224 | tf_op jit(solution)/shard_map/ppermute | solution.py:50
  117.3 7.8 %collective-permute-start.26 = (bf16[256,256]{1,0:T(8,128)(2,1)S(1)}, bf16[256,256]{1,0:T(8,128)(2,1)S(1)}, u32[]{:S(2)}, u32[]{:S(2)}) collective-permute-start(bf16[256,256]{1,0:T(8,128)(2,1)S(1)} %get-tuple-element.44), channel_id=1, source_target_pairs={{0,8},{2,10},{4,12},{6,14},{8,0},{10,2},{12,4},{14,6},{16,24},{18,... | collective-permute-start | bytes 393224 | tf_op jit(solution)/shard_map/ppermute | solution.py:50
  (4 other events, 7.7 us)

commit v2 on v1

v2 whole, which is shorter than its diff:
```python
import functools

import jax
import jax.numpy as jnp
from jax import lax
from jax.experimental import pallas as pl
from jax.experimental.pallas import tpu as pltpu
from jax.sharding import PartitionSpec as P

DK = 128
BLOCK = 128

absmean_eps = 1e-05
norm_eps = 1e-06

BF16 = jnp.bfloat16
F32 = jnp.float32
VMEM_LIMIT = 20 * 1024 * 1024


def rows_by_rows(a, b):
    return lax.dot_general(a, b, (((0,), (0,)), ((), ())), preferred_element_type=F32)


def by_rows(a, b):
    return lax.dot_general(a, b, (((1,), (1,)), ((), ())), preferred_element_type=F32)


def plain(a, b):
    return jnp.dot(a, b, preferred_element_type=F32)


def block_rows(i):
    return slice(i * BLOCK, (i + 1) * BLOCK)


def causal_mask():
    at = lax.broadcasted_iota(jnp.int32, (BLOCK, BLOCK), 0)
    of = lax.broadcasted_iota(jnp.int32, (BLOCK, BLOCK), 1)
    return at >= of


def place():
    s = lax.axis_index("seq")
    return lax.rem(s, 2), lax.div(s, 2), lax.axis_index("head")


def swap(array, axis, distance):
    count = lax.axis_size(axis)
    return lax.ppermute(array, axis, [(i, i ^ distance) for i in range(count)])


EXTRA = 16


def slab_kernel(latent_ref, sums_ref, got_ref, out_ref):
    rows, columns = latent_ref.shape
    out_ref[:rows, :] = latent_ref[...].astype(BF16)
    rest = sums_ref[...] + got_ref[...]
    row = lax.broadcasted_iota(jnp.int32, (EXTRA, columns), 0)
    tail = jnp.zeros((EXTRA, columns), F32)
    for i in range(3):
        part = rest.astype(BF16).astype(F32)
        tail = jnp.where(row == i, part, tail)
        rest = rest - part
    out_ref[rows:, :] = tail.astype(BF16)


def project(piece_refs, w_ref, keep_ref, send_ref):
    side, _, head = place()
    width = piece_refs[0].shape[1]
    p = None
    for k, ref in enumerate(piece_refs):
        part = w_ref[pl.ds(pl.multiple_of((head ^ k) * width, width), width), :]
        term = plain(ref[...], part)
        p = term if p is None else p + term
    keep_ref[...] = jnp.where(side == 0, p[:, :DK], p[:, DK:])
    send_ref[...] = jnp.where(side == 0, p[:, DK:], p[:, :DK]).astype(BF16)


def project_own_kernel(far, slabs, total_rows, *refs):
    slab_refs, piece_refs = refs[:slabs], refs[slabs:-5]
    w_ref, keep_ref, send_ref, slabs_ref, sems = refs[-5:]
    copies = [
        pltpu.make_async_copy(a, slabs_ref.at[i], sems.at[i]) for i, a in enumerate(slab_refs)
    ]
    for copy in copies:
        copy.start()
    for copy in copies:
        copy.wait()
    _, pair, _ = place()
    rows = slab_refs[0].shape[0] - EXTRA
    sums = jnp.sum(slabs_ref[:, rows:, :].astype(F32), axis=0)
    scale = jnp.sum(sums, axis=0, keepdims=True) / total_rows + absmean_eps
    halfway = 0.5 * scale
    for i in range(slabs):
        r = 2 * i if i < far else 2 * (i - far) + 1
        w = slabs_ref[i, :rows, :].astype(F32)
        signs = jnp.where(w > halfway, scale, jnp.where(w < -halfway, -scale, 0.0))
        w_ref[pl.ds(pl.multiple_of((pair ^ r) * rows, rows), rows), :] = signs.astype(BF16)
    project(piece_refs, w_ref, keep_ref, send_ref)


def project_got_kernel(w_ref, *refs):
    project(refs[:-2], w_ref, *refs[-2:])


def park_kernel(n, *refs):
    copies = [pltpu.make_async_copy(refs[i], refs[n + 1 + i], refs[-1].at[i]) for i in range(n)]
    for copy in copies:
        copy.start()
    for copy in copies:
        copy.wait()


def park(arrays, after):
    n = len(arrays)
    return pl.pallas_call(
        functools.partial(park_kernel, n),
        out_shape=[pltpu.HBM(a.shape, a.dtype) for a in arrays],
        in_specs=vmem_specs(n) + [pl.BlockSpec(memory_space=pl.ANY)],
        out_specs=[pl.BlockSpec(memory_space=pltpu.HBM)] * n,
        scratch_shapes=[pltpu.SemaphoreType.DMA((n,))],
        compiler_params=pltpu.CompilerParams(vmem_limit_bytes=VMEM_LIMIT),
    )(*arrays, after)


def vmem_specs(n):
    return [pl.BlockSpec(memory_space=pltpu.VMEM)] * n


def call(kernel, outs, args, flops, scratch=(), specs=None):
    size = sum(a.size * a.dtype.itemsize for a in args)
    size += sum(o.size * o.dtype.itemsize for o in outs)
    return pl.pallas_call(
        kernel,
        out_shape=outs,
        in_specs=specs or vmem_specs(len(args)),
        out_specs=vmem_specs(len(outs)),
        scratch_shapes=list(scratch),
        compiler_params=pltpu.CompilerParams(vmem_limit_bytes=VMEM_LIMIT),
        cost_estimate=pl.CostEstimate(flops=flops, bytes_accessed=size, transcendentals=0),
    )(*args)


def shape(dims, dtype):
    return jax.ShapeDtypeStruct(dims, dtype)


def values_kernel(own_ref, own_got_ref, got_ref, got_got_ref, k_ref, v_ref, total_ref, total16_ref):
    side, _, _ = place()
    tokens = own_ref.shape[0]
    own = (own_ref[...] + own_got_ref[...].astype(F32)).astype(BF16)
    got = (got_ref[...] + got_got_ref[...].astype(F32)).astype(BF16)
    v_ref[pl.ds(pl.multiple_of(side * tokens, tokens), tokens), :] = own
    v_ref[pl.ds(pl.multiple_of((1 - side) * tokens, tokens), tokens), :] = got
    total = rows_by_rows(k_ref[...], v_ref[...])
    total_ref[...] = total
    total16_ref[...] = total.astype(BF16)


def intra_kernel(blocks, q_ref, k_ref, v_ref, mixed_ref, local_ref):
    mask = causal_mask()
    state = jnp.zeros((DK, DK), F32)
    for i in range(blocks):
        q, k, v = (ref[block_rows(i), :] for ref in (q_ref, k_ref, v_ref))
        scores = jnp.where(mask, by_rows(q, k), 0.0).astype(BF16)
        earlier = state.astype(BF16)
        local_ref[i] = earlier
        mixed_ref[block_rows(i), :] = plain(scores, v) + plain(q, earlier)
        if i < blocks - 1:
            state = state + rows_by_rows(k, v)


def norm_kernel(mixed_ref, prior_ref, q_ref, up_ref, out_ref, gm_ref, total_ref, total16_ref):
    q = q_ref[...]
    mixed = mixed_ref[...] + plain(q, prior_ref[...].astype(BF16))
    inverse = lax.rsqrt(jnp.mean(mixed * mixed, axis=-1, keepdims=True) + norm_eps)
    normed = mixed * inverse
    out_ref[...] = normed.astype(BF16)
    up = up_ref[...].astype(F32)
    inner = jnp.mean(up * normed, axis=-1, keepdims=True)
    gm = ((up - normed * inner) * inverse).astype(BF16)
    gm_ref[...] = gm
    total = rows_by_rows(q, gm)
    total_ref[...] = total
    total16_ref[...] = total.astype(BF16)


def local_grad_kernel(
    blocks, q_ref, k_ref, v_ref, gm_ref, local_ref, prior_ref, gq_ref, gk_ref, gv_ref, gv16_ref
):
    mask = causal_mask()
    state = jnp.zeros((DK, DK), F32)
    for i in reversed(range(blocks)):
        q, k, v, gm = (ref[block_rows(i), :] for ref in (q_ref, k_ref, v_ref, gm_ref))
        scores = jnp.where(mask, by_rows(q, k), 0.0).astype(BF16)
        gscores = jnp.where(mask, by_rows(gm, v), 0.0).astype(BF16)
        later = state.astype(BF16)
        prior = (prior_ref[...] + local_ref[i].astype(F32)).astype(BF16)
        gq_ref[block_rows(i), :] = (plain(gscores, k) + by_rows(gm, prior)).astype(BF16)
        gk_ref[block_rows(i), :] = rows_by_rows(gscores, q) + by_rows(v, later)
        gv = rows_by_rows(scores, gm) + plain(k, later)
        gv_ref[block_rows(i), :] = gv
        gv16_ref[block_rows(i), :] = gv.astype(BF16)
        if i:
            state = state + rows_by_rows(q, gm)


def grad_key_kernel(gk_ref, v_ref, after_ref, out_ref):
    out_ref[...] = (gk_ref[...] + by_rows(v_ref[...], after_ref[...])).astype(BF16)


def latent_part(sent, piece_refs, g_ref, out_ref):
    _, pair, head = place()
    width = piece_refs[0].shape[1]
    rows = out_ref.shape[-1]
    chunks = width // rows
    odd = lax.rem(pair, 2) ^ sent
    for k in range(len(piece_refs) // 2):
        for c in range(0, chunks, 2):
            part = None
            for t in range(2):
                two = piece_refs[2 * k + t][:, c * rows : (c + 2) * rows]
                one = jnp.where(odd == 0, two[:, :rows], two[:, rows:])
                term = plain(g_ref[t], one)
                part = term if part is None else part + term
            slab = (head ^ k) * chunks + c + odd
            out_ref[lax.div(pair ^ slab, 2)] = part.astype(out_ref.dtype)


def latent_send_kernel(gv_ref, k_ref, after_ref, got_ref, k_got_ref, after_got_ref, *refs):
    piece_refs = refs[:-2]
    out_ref, g_ref = refs[-2:]
    side, _, _ = place()
    tokens = piece_refs[0].shape[0]
    after, after_got = after_ref[...], after_got_ref[...]
    for t in range(2):
        at = pl.ds(pl.multiple_of((side ^ t) * tokens, tokens), tokens)
        own = gv_ref[at, :] + plain(k_ref[at, :], after)
        got = got_ref[at, :].astype(F32) + plain(k_got_ref[at, :], after_got)
        g_ref[t, :DK, :] = jnp.where(side == 0, own, got).T.astype(BF16)
        g_ref[t, DK:, :] = jnp.where(side == 0, got, own).T.astype(BF16)
    latent_part(1, piece_refs, g_ref, out_ref)


def latent_keep_kernel(g_ref, *refs):
    latent_part(0, refs[:-1], g_ref, refs[-1])


def join_kernel(i, keep_ref, got_ref, out_ref):
    out_ref[...] = (keep_ref[i] + got_ref[...].astype(F32)).astype(BF16)


def sum_kernel(n, *refs):
    total = refs[0][0]
    for ref in refs[1:n]:
        total = total + ref[...].astype(F32)
    refs[n][...] = total.T


def in_hbm(array):
    return pltpu.with_memory_space_constraint(array, pltpu.HBM)


def pick(flag, even, odd):
    return jnp.where(flag == 0, even, odd)


def per_device(inputs, latent, queries, keys, grad_out):
    n, heads = lax.axis_size("seq"), lax.axis_size("head")
    side, pair, head = place()
    rows, columns = latent.shape
    tokens = inputs.shape[0]
    pairs, far = n // 2, n // 4
    blocks = 2 * tokens // BLOCK

    def half(flag):
        chunks = [
            pick(flag, inputs[:, 2 * c * rows :][:, :rows], inputs[:, (2 * c + 1) * rows :][:, :rows])
            for c in range(inputs.shape[1] // (2 * rows))
        ]
        return jnp.concatenate(chunks, axis=1)

    sums = jnp.sum(jnp.abs(latent), axis=0, keepdims=True)
    got_sums = swap(sums, "seq", 1)
    sent_half, got_sums = lax.optimization_barrier((half(1 - side), got_sums))
    got_half = swap(sent_half, "seq", 1)
    own_half = half(side)

    (slab,) = call(slab_kernel, [shape((rows + EXTRA, columns), BF16)], [latent, sums, got_sums], 0)
    even = [slab] + [None] * (far - 1)
    odd = [swap(slab, "seq", 2)] + [None] * (far - 1)
    for i in range(2, far):
        even[i] = swap(slab, "seq", 4 * i)
    even[2:], odd[0], slab_late = lax.optimization_barrier((even[2:], odd[0], slab))
    for i in range(2, far):
        odd[i] = swap(even[i], "seq", 2)
    if far > 1:
        even[1] = swap(slab_late, "seq", 4)
        odd[1] = swap(even[1], "seq", 2)
    slab_list = even + odd
    own_late, _ = lax.optimization_barrier((own_half, even[-1]))
    own_pieces = [own_half] + [swap(own_late, "head", k) for k in range(1, heads)]
    half_cost = 2 * tokens * pairs * rows * columns
    weights, keep_own, send_own = call(
        functools.partial(project_own_kernel, far, len(slab_list), n * rows),
        [
            shape((pairs * rows, columns), BF16),
            shape((tokens, DK), F32),
            shape((tokens, DK), BF16),
        ],
        [in_hbm(a) for a in slab_list] + own_pieces,
        half_cost,
        [pltpu.VMEM((pairs, *slab.shape), BF16), pltpu.SemaphoreType.DMA((pairs,))],
        [pl.BlockSpec(memory_space=pl.ANY)] * pairs + vmem_specs(heads),
    )
    got_late, _ = lax.optimization_barrier((got_half, odd))
    keys_late, _ = lax.optimization_barrier((keys, even[-1]))
    got_pieces = [got_half] + [swap(got_late, "head", k) for k in range(1, heads)]
    keep_got, send_got = call(
        project_got_kernel,
        [shape((tokens, DK), F32), shape((tokens, DK), BF16)],
        [weights] + got_pieces,
        half_cost,
    )
    values_got, values_own = swap(send_own, "seq", 1), swap(send_got, "seq", 1)
    pieces = [a for two in zip(own_pieces, got_pieces) for a in two]

    def part_of(array, flag):
        return pick(flag, array[:, :DK], array[:, DK:])

    def joined(mine, theirs, late):
        mine, theirs, _ = lax.optimization_barrier((mine, theirs, late))
        return jnp.concatenate([pick(side, mine, theirs), pick(side, theirs, mine)], axis=0)

    k = joined(part_of(keys_late, side), swap(part_of(keys_late, 1 - side), "seq", 1), send_got)
    long = 2 * tokens
    cost = 2 * long * DK * DK
    v, total, total16 = call(
        values_kernel,
        [shape((long, DK), BF16), shape((DK, DK), F32), shape((DK, DK), BF16)],
        [keep_own, values_own, keep_got, values_got, k],
        cost,
    )
    parked = list(park(pieces, v))
    queries_late, up_late, keys_later, _ = lax.optimization_barrier(
        (queries, grad_out, keys, send_got)
    )
    early = [
        (part_of(a, side), swap(part_of(a, 1 - side), "seq", 1)) for a in (queries_late, up_late)
    ]
    k_parts = part_of(keys_later, 1 - side), swap(part_of(keys_later, side), "seq", 1)

    def scan(total, total16, backward, hooks):
        before = jnp.zeros_like(total)
        distance, at, results = 1, 0, []
        while distance < pairs:
            got = swap(total16, "seq", 2 * distance).astype(F32)
            high = lax.rem(lax.div(pair, distance), 2) == (0 if backward else 1)
            before = before + jnp.where(high, got, 0.0)
            if at < len(hooks):
                result = hooks[at](total16)
            total = total + got
            total16 = total.astype(BF16)
            if at < len(hooks):
                total16, result = lax.optimization_barrier((total16, result))
                results.append(result)
            distance, at = distance * 2, at + 1
        return before, results

    def intra():
        return call(
            functools.partial(intra_kernel, blocks),
            [shape((long, DK), F32), shape((blocks, DK, DK), BF16)],
            [q, k, v],
            4 * cost,
        )

    prior, (pieces, (q, up)) = scan(
        total,
        total16,
        False,
        [lambda _: parked, lambda late: [joined(*a, late) for a in early]],
    )
    mixed, local_prior = intra()
    out, gm, gtotal, gtotal16 = call(
        norm_kernel,
        [
            shape((long, DK), BF16),
            shape((long, DK), BF16),
            shape((DK, DK), F32),
            shape((DK, DK), BF16),
        ],
        [mixed, prior, q, up],
        2 * cost,
    )

    def local_grads():
        return call(
            functools.partial(local_grad_kernel, blocks),
            [
                shape((long, DK), BF16),
                shape((long, DK), F32),
                shape((long, DK), F32),
                shape((long, DK), BF16),
            ],
            [q, k, v, gm, local_prior, prior],
            9 * cost,
        )

    local = local_grads()
    after, ((_, (gq, gk_part, gv_part, gv16)), k_got) = scan(
        gtotal, gtotal16, True, [lambda _: ((), local), lambda late: joined(*k_parts, late)]
    )
    gv_got = swap(gv16, "seq", 1)
    after16 = after.astype(BF16)
    after16, gv_got = lax.optimization_barrier((after16, gv_got))
    after_got = swap(after16, "seq", 1)
    half_slabs = (far, columns, rows)
    send_parts, gv_both = call(
        latent_send_kernel,
        [shape(half_slabs, BF16), shape((2, columns, tokens), BF16)],
        [gv_part, k, after16, gv_got, k_got, after_got] + pieces,
        half_cost + 2 * cost,
    )
    (keep_parts,) = call(
        latent_keep_kernel, [shape(half_slabs, F32)], [gv_both] + pieces, half_cost
    )
    after_late, _ = lax.optimization_barrier((after16, send_parts))
    (gk,) = call(grad_key_kernel, [shape((long, DK), BF16)], [gk_part, v, after_late], cost)

    arrived = []
    for i in reversed(range(1, far)):
        (joined,) = call(
            functools.partial(join_kernel, i),
            [shape((columns, rows), BF16)],
            [keep_parts, swap(send_parts[i], "seq", 2)],
            0,
        )
        arrived.append(swap(joined, "seq", 4 * i))
    terms = [keep_parts, swap(send_parts[0], "seq", 2)] + arrived
    def token_half(flag):
        return jnp.stack([pick(flag, a[:tokens], a[tokens:]) for a in (out, gq, gk)])

    mine, theirs = token_half(side), swap(token_half(1 - side), "seq", 1)
    attn_out, grad_queries, grad_keys = (
        jnp.concatenate([pick(side, mine[i], theirs[i]), pick(side, theirs[i], mine[i])], axis=1)
        for i in range(3)
    )
    outs, terms = lax.optimization_barrier(((attn_out, grad_queries, grad_keys), terms))
    (grad_latent,) = call(
        functools.partial(sum_kernel, len(terms)), [shape((rows, columns), F32)], terms, 0
    )
    return (*outs, grad_latent)


def solution(mesh):
    placed = (P("seq", "head"),) * 5
    return jax.shard_map(
        per_device,
        mesh=mesh,
        in_specs=placed,
        out_specs=(P("seq", "head"),) * 4,
        check_vma=False,
    )
```

time: 126 us -> 99.3 us (0.79)
  waiting for transfers between devices: 56.2 us -> 38.8 us
  blocking collectives: 12.2 us -> 0 us
  starting transfers between devices: 33.2 us -> 40.7 us
  other arithmetic: 7.67 us -> 5.65 us
  local copies, waits for them, and re-layouts: 1.75 us -> 0.11 us
    ppermute x27 -> x33, waiting for transfers between devices: 56.2 us -> 38.8 us  [swap(): return lax.ppermute(array, axis, [(i, i ^ distance) for i in range(count)])]
    all_to_all x1 -> x0, blocking collectives: 12.2 us -> none  [per_device(): lax.all_to_all(jnp.broadcast_to(sums[None], (n, columns)), 'seq', 0, 0, t...]
    ppermute x27 -> x33, starting transfers between devices: 33.2 us -> 40.7 us  [swap(): return lax.ppermute(array, axis, [(i, i ^ distance) for i in range(count)])]
    pallas_call x9 -> x14, Pallas kernels: 13.9 us -> 10.8 us  [call(): pl.pallas_call(kernel, out_shape=outs, in_specs=specs or vmem_specs(len(a...]
    convert_element_type x4, other arithmetic: 2.19 us -> 0.05 us  [scan(): total16 = total.astype(BF16)]
    pallas_call x0 -> x1, Pallas kernels: none -> 2.02 us  [park(): pl.pallas_call(functools.partial(park_kernel, n), out_shape=[pltpu.HBM(a....]
    unnamed x19 -> x32, local copies, waits for them, and re-layouts: 1.68 us -> 0.07 us
  transfers between devices with their start and end apart: 27 -> 33, of which waited for: 15 -> 17; matrix products, arithmetic and copies ran while one was open for 2% -> 5% of each run, Pallas kernels for 9% -> 10%
where the time goes in v2:
time: 99.3 us; the launch traced here: 99.1 us
  starting transfers between devices  40.7 us (41%)
  waiting for transfers between devices  38.8 us (39%)
  Pallas kernels  12.8 us (13%)
  other arithmetic  5.65 us (6%)
  between operations  1.06 us (1%)
    ppermute x33, starting transfers between devices, swap(): return lax.ppermute(array, axis, [(i, i ^ distance) for i in range(count)])  40.7 us
    ppermute x33, waiting for transfers between devices, swap(): return lax.ppermute(array, axis, [(i, i ^ distance) for i in range(count)])  38.8 us
    pallas_call x14, Pallas kernels, call(): pl.pallas_call(kernel, out_shape=outs, in_specs=specs or vmem_specs(len(a...  10.8 us
    concatenate x3, other arithmetic, per_device(): jnp.concatenate([pick(side, mine[i], theirs[i]), pick(side, theirs[i], mi...  2.2 us
    pallas_call x1, Pallas kernels, park(): pl.pallas_call(functools.partial(park_kernel, n), out_shape=[pltpu.HBM(a....  2.02 us
  transfers between devices with their start and end apart: 33, of which 17 were waited for; matrix products, arithmetic and copies ran while one was open for 5% of the time, Pallas kernels for 10%

profile of v2, /device:TPU:0, one launch (start us, length us, event | category | flops | bytes accessed | tf_op | source)
XLA Modules:
  0.0 99.1 jit_solution(11028934224770365013)
XLA Ops:
  1.6 3.0 %collective-permute-start = (f32[1,256]{1,0:T(1,128)S(1)}, f32[1,256]{1,0:T(1,128)S(1)}, u32[]{:S(2)}, u32[]{:S(2)}) collective-permute-start(f32[1,256]{1,0:T(1,128)S(1)} %bitcast.33), channel_id=1, source_target_pairs={{0,2},{2,0},{4,6},{6,4},{8,10},{10,8},{12,14},{14,12},{16,18},{18,... | collective-permute-start | bytes 3080 | tf_op jit(solution)/shard_map/ppermute | solution.py:50
  4.6 1.7 %broadcast_select_fusion.3 = (bf16[512,256]{1,0:T(8,128)(2,1)S(1)}, bf16[512,256]{1,0:T(8,128)(2,1)S(1)}, bf16[512,256]{1,0:T(8,128)(2,1)S(1)}, bf16[512,256]{1,...) fusion(pred[]{:T(512)S(6)} %eq.16, ...), kind=kLoop, calls=%fused_computation.14 | loop fusion | flops 1048576 | bytes 4194306 | tf_op jit(solution)/shard_map/jit(_where)/select_n | solution.py:267
  6.5 1.7 %collective-permute-start.9 = (bf16[512,1024]{1,0:T(8,128)(2,1)S(1)}, bf16[512,1024]{1,0:T(8,128)(2,1)S(1)}, u32[]{:S(2)}, u32[]{:S(2)}) collective-permute-start(bf16[512,1024]{1,0:T(8,128)(2,1)S(1)} %pad_maximum_fusion), channel_id=1, source_target_pairs={{0,2},{2,0},{4,6},{6,4},{8,10},{10,8},{12,14},{14,12},{16,18},{18,... | collective-permute-start | bytes 3145736 | tf_op jit(solution)/shard_map/ppermute | solution.py:50
  8.2 1.6 %collective-permute-start.3 = (bf16[272,256]{1,0:T(8,128)(2,1)S(1)}, bf16[272,256]{1,0:T(8,128)(2,1)S(1)}, u32[]{:S(2)}, u32[]{:S(2)}) collective-permute-start(bf16[272,256]{1,0:T(8,128)(2,1)S(1)} %shard_map.84.refs_0_), channel_id=1, source_target_pairs={{0,4},{2,6},{4,0},{6,2},{8,12},{10,14},{12,8},{14,10},{16,20},{18,... | collective-permute-start | bytes 417800 | tf_op jit(solution)/shard_map/ppermute | solution.py:50
  9.8 3.6 %collective-permute-start.2 = (bf16[272,256]{1,0:T(8,128)(2,1)S(1)}, bf16[272,256]{1,0:T(8,128)(2,1)S(1)}, u32[]{:S(2)}, u32[]{:S(2)}) collective-permute-start(bf16[272,256]{1,0:T(8,128)(2,1)S(1)} %shard_map.84.refs_0_), channel_id=1, source_target_pairs={{0,24},{2,26},{4,28},{6,30},{8,16},{10,18},{12,20},{14,22},{16,8},... | collective-permute-start | bytes 417800 | tf_op jit(solution)/shard_map/ppermute | solution.py:50
  13.4 3.7 %collective-permute-done.2.refs_3_ = bf16[272,256]{1,0:T(8,128)(2,1)S(1)} collective-permute-done((bf16[272,256]{1,0:T(8,128)(2,1)S(1)}, bf16[272,256]{1,0:T(8,128)(2,1)S(1)}, u32[]{:S(2)}, u32[]{:S(2)}) %collective-permute-start.2) | collective-permute-done | bytes 139296 | tf_op jit(solution)/shard_map/ppermute | solution.py:50
  17.2 6.5 %collective-permute-done.1.refs_2_ = bf16[272,256]{1,0:T(8,128)(2,1)S(1)} collective-permute-done((bf16[272,256]{1,0:T(8,128)(2,1)S(1)}, bf16[272,256]{1,0:T(8,128)(2,1)S(1)}, u32[]{:S(2)}, u32[]{:S(2)}) %collective-permute-start.1) | collective-permute-done | bytes 139296 | tf_op jit(solution)/shard_map/ppermute | solution.py:50
  24.2 1.5 %collective-permute-start.7 = (bf16[272,256]{1,0:T(8,128)(2,1)S(1)}, bf16[272,256]{1,0:T(8,128)(2,1)S(1)}, u32[]{:S(2)}, u32[]{:S(2)}) collective-permute-start(bf16[272,256]{1,0:T(8,128)(2,1)S(1)} %collective-permute-done.2.refs_3_), channel_id=1, source_target_pairs={{0,4},{2,6},{4,0},{6,2},{8,12},{10,14},{12,8},{14,10},{16,20},{18,... | collective-permute-start | bytes 417800 | tf_op jit(solution)/shard_map/ppermute | solution.py:50
  25.7 3.0 %collective-permute-done.4.refs_1_ = bf16[272,256]{1,0:T(8,128)(2,1)S(1)} collective-permute-done((bf16[272,256]{1,0:T(8,128)(2,1)S(1)}, bf16[272,256]{1,0:T(8,128)(2,1)S(1)}, u32[]{:S(2)}, u32[]{:S(2)}) %collective-permute-start.4) | collective-permute-done | bytes 139296 | tf_op jit(solution)/shard_map/ppermute | solution.py:50
  30.1 2.8 %collective-permute-done.7.refs_7_ = bf16[272,256]{1,0:T(8,128)(2,1)S(1)} collective-permute-done((bf16[272,256]{1,0:T(8,128)(2,1)S(1)}, bf16[272,256]{1,0:T(8,128)(2,1)S(1)}, u32[]{:S(2)}, u32[]{:S(2)}) %collective-permute-start.7) | collective-permute-done | bytes 139296 | tf_op jit(solution)/shard_map/ppermute | solution.py:50
  32.9 1.5 %collective-permute-done.5.refs_5_ = bf16[272,256]{1,0:T(8,128)(2,1)S(1)} collective-permute-done((bf16[272,256]{1,0:T(8,128)(2,1)S(1)}, bf16[272,256]{1,0:T(8,128)(2,1)S(1)}, u32[]{:S(2)}, u32[]{:S(2)}) %collective-permute-start.5) | collective-permute-done | bytes 139296 | tf_op jit(solution)/shard_map/ppermute | solution.py:50
  35.6 2.8 %shard_map.85 = (bf16[2048,256]{1,0:T(8,128)(2,1)S(1)}, f32[512,128]{1,0:T(8,128)S(1)}, bf16[512,128]{1,0:T(8,128)(2,1)S(1)}) custom-call(bf16[272,256]{1,0:T(8,128)(2,1)} %copy-done.5, bf16[272,256]{1,0:T(8,128)(2,1)} %copy-done.12, bf16[272,256]{1,0:T(8,128)(2,1)} %copy-done.11, bf16[272,256]{1,0:T(8,128)(2,1)} %copy-done.10, bf16[272,256]{1,0:T(8,128)(2,1)} %copy-done.9, ...), custom_call_target="tpu_custom_call" | custom-call | flops 536870912 | bytes 4653056 | tf_op jit(solution)/shard_map/pallas_call | solution.py:135
  42.4 2.4 %collective-permute-done.12.got_got_ref = bf16[512,128]{1,0:T(8,128)(2,1)S(1)} collective-permute-done((bf16[512,128]{1,0:T(8,128)(2,1)S(1)}, bf16[512,128]{1,0:T(8,128)(2,1)S(1)}, u32[]{:S(2)}, u32[]{:S(2)}) %collective-permute-start.12) | collective-permute-done | bytes 131104 | tf_op jit(solution)/shard_map/ppermute | solution.py:50
  44.8 2.8 %collective-permute-done.11.own_got_ref = bf16[512,128]{1,0:T(8,128)(2,1)S(1)} collective-permute-done((bf16[512,128]{1,0:T(8,128)(2,1)S(1)}, bf16[512,128]{1,0:T(8,128)(2,1)S(1)}, u32[]{:S(2)}, u32[]{:S(2)}) %collective-permute-start.11) | collective-permute-done | bytes 131104 | tf_op jit(solution)/shard_map/ppermute | solution.py:50
  49.6 2.0 %shard_map.88 = (bf16[512,1024]{1,0:T(8,128)(2,1)}, bf16[512,1024]{1,0:T(8,128)(2,1)}, bf16[512,1024]{1,0:T(8,128)(2,1)}, bf16[512,1024]{1,0:T(8,128)(2,1)}) custom-call(bf16[512,1024]{1,0:T(8,128)(2,1)S(1)} %pad_maximum_fusion.1.refs_8_.refs_0_, bf16[512,1024]{1,0:T(8,128)(2,1)S(1)} %collective-permute-done.9.refs_0_.refs_1_, ...), custom_call_target="tpu_custom_call" | custom-call | tf_op jit(solution)/shard_map/pallas_call | solution.py:118
  51.9 1.8 %collective-permute-start.15 = (bf16[128,128]{1,0:T(8,128)(2,1)S(1)}, bf16[128,128]{1,0:T(8,128)(2,1)S(1)}, u32[]{:S(2)}, u32[]{:S(2)}) collective-permute-start(bf16[128,128]{1,0:T(8,128)(2,1)S(1)} %fusion.7), channel_id=1, source_target_pairs={{0,8},{2,10},{4,12},{6,14},{8,0},{10,2},{12,4},{14,6},{16,24},{18,... | collective-permute-start | bytes 98312 | tf_op jit(solution)/shard_map/ppermute | solution.py:50
  53.9 2.1 %collective-permute-done.15 = bf16[128,128]{1,0:T(8,128)(2,1)S(1)} collective-permute-done((bf16[128,128]{1,0:T(8,128)(2,1)S(1)}, bf16[128,128]{1,0:T(8,128)(2,1)S(1)}, u32[]{:S(2)}, u32[]{:S(2)}) %collective-permute-start.15) | collective-permute-done | bytes 32800 | tf_op jit(solution)/shard_map/ppermute | solution.py:50
  55.9 1.5 %collective-permute-start.18 = (bf16[128,128]{1,0:T(8,128)(2,1)S(1)}, bf16[128,128]{1,0:T(8,128)(2,1)S(1)}, u32[]{:S(2)}, u32[]{:S(2)}) collective-permute-start(bf16[128,128]{1,0:T(8,128)(2,1)S(1)} %fusion.2), channel_id=1, source_target_pairs={{0,16},{2,18},{4,20},{6,22},{8,24},{10,26},{12,28},{14,30},{16,0},... | collective-permute-start | bytes 98312 | tf_op jit(solution)/shard_map/ppermute | solution.py:50
  57.4 1.4 %shard_map.89 = (f32[1024,128]{1,0:T(8,128)S(1)}, bf16[8,128,128]{2,1,0:T(8,128)(2,1)S(1)}) custom-call(bf16[1024,128]{1,0:T(8,128)(2,1)S(1)} %get-tuple-element.104.q_ref, bf16[1024,128]{1,0:T(8,128)(2,1)S(1)} %pad_maximum_fusion.3.k_ref, bf16[1024,128]{1,0:T(8,128)(2,1)S(1)} %get-tuple-element.92.refs_4_.v_ref), custom_call_target="tpu_custom_call" | custom-call | flops 134217728 | bytes 1572864 | tf_op jit(solution)/shard_map/pallas_call | solution.py:135
  58.8 2.0 %collective-permute-done.18 = bf16[128,128]{1,0:T(8,128)(2,1)S(1)} collective-permute-done((bf16[128,128]{1,0:T(8,128)(2,1)S(1)}, bf16[128,128]{1,0:T(8,128)(2,1)S(1)}, u32[]{:S(2)}, u32[]{:S(2)}) %collective-permute-start.18) | collective-permute-done | bytes 32800 | tf_op jit(solution)/shard_map/ppermute | solution.py:50
  61.6 1.3 %collective-permute-start.19 = (bf16[128,128]{1,0:T(8,128)(2,1)S(1)}, bf16[128,128]{1,0:T(8,128)(2,1)S(1)}, u32[]{:S(2)}, u32[]{:S(2)}) collective-permute-start(bf16[128,128]{1,0:T(8,128)(2,1)S(1)} %get-tuple-element.110), channel_id=1, source_target_pairs={{0,4},{2,6},{4,0},{6,2},{8,12},{10,14},{12,8},{14,10},{16,20},{18,... | collective-permute-start | bytes 98312 | tf_op jit(solution)/shard_map/ppermute | solution.py:50
  64.0 1.9 %shard_map.91 = (bf16[1024,128]{1,0:T(8,128)(2,1)S(1)}, f32[1024,128]{1,0:T(8,128)S(1)}, f32[1024,128]{1,0:T(8,128)S(1)}, bf16[1024,128]{1,0:T(8,128)(2,1)S(1)}) custom-call(bf16[1024,128]{1,0:T(8,128)(2,1)S(1)} %get-tuple-element.104.q_ref, bf16[1024,128]{1,0:T(8,128)(2,1)S(1)} %pad_maximum_fusion.3.k_ref, ...), custom_call_target="tpu_custom_call" | custom-call | flops 301989888 | bytes 2949120 | tf_op jit(solution)/shard_map/pallas_call | solution.py:135
  66.0 2.1 %collective-permute-start.20 = (bf16[128,128]{1,0:T(8,128)(2,1)S(1)}, bf16[128,128]{1,0:T(8,128)(2,1)S(1)}, u32[]{:S(2)}, u32[]{:S(2)}) collective-permute-start(bf16[128,128]{1,0:T(8,128)(2,1)S(1)} %fusion.8), channel_id=1, source_target_pairs={{0,8},{2,10},{4,12},{6,14},{8,0},{10,2},{12,4},{14,6},{16,24},{18,... | collective-permute-start | bytes 98312 | tf_op jit(solution)/shard_map/ppermute | solution.py:50
  68.1 1.3 %collective-permute-done.21 = bf16[512,128]{1,0:T(8,128)(2,1)S(1)} collective-permute-done((bf16[512,128]{1,0:T(8,128)(2,1)S(1)}, bf16[512,128]{1,0:T(8,128)(2,1)S(1)}, u32[]{:S(2)}, u32[]{:S(2)}) %collective-permute-start.21) | collective-permute-done | bytes 131104 | tf_op jit(solution)/shard_map/ppermute | solution.py:50
  70.5 1.5 %collective-permute-start.22 = (bf16[128,128]{1,0:T(8,128)(2,1)S(1)}, bf16[128,128]{1,0:T(8,128)(2,1)S(1)}, u32[]{:S(2)}, u32[]{:S(2)}) collective-permute-start(bf16[128,128]{1,0:T(8,128)(2,1)S(1)} %fusion.6), channel_id=1, source_target_pairs={{0,16},{2,18},{4,20},{6,22},{8,24},{10,26},{12,28},{14,30},{16,0},... | collective-permute-start | bytes 98312 | tf_op jit(solution)/shard_map/ppermute | solution.py:50
  72.0 3.4 %collective-permute-done.22 = bf16[128,128]{1,0:T(8,128)(2,1)S(1)} collective-permute-done((bf16[128,128]{1,0:T(8,128)(2,1)S(1)}, bf16[128,128]{1,0:T(8,128)(2,1)S(1)}, u32[]{:S(2)}, u32[]{:S(2)}) %collective-permute-start.22) | collective-permute-done | bytes 32800 | tf_op jit(solution)/shard_map/ppermute | solution.py:50
  76.8 3.3 %collective-permute-done.24.after_got_ref = bf16[128,128]{1,0:T(8,128)(2,1)S(1)} collective-permute-done((bf16[128,128]{1,0:T(8,128)(2,1)S(1)}, bf16[128,128]{1,0:T(8,128)(2,1)S(1)}, u32[]{:S(2)}, u32[]{:S(2)}) %collective-permute-start.24) | collective-permute-done | bytes 32800 | tf_op jit(solution)/shard_map/ppermute | solution.py:50
  83.4 1.3 %collective-permute-start.29 = (bf16[256,256]{1,0:T(8,128)(2,1)S(1)}, bf16[256,256]{1,0:T(8,128)(2,1)S(1)}, u32[]{:S(2)}, u32[]{:S(2)}) collective-permute-start(bf16[256,256]{1,0:T(8,128)(2,1)S(1)} %get-tuple-element.159), channel_id=1, source_target_pairs={{0,4},{2,6},{4,0},{6,2},{8,12},{10,14},{12,8},{14,10},{16,20},{18,... | collective-permute-start | bytes 393224 | tf_op jit(solution)/shard_map/ppermute | solution.py:50
  85.4 1.3 %collective-permute-start.26 = (bf16[256,256]{1,0:T(8,128)(2,1)S(1)}, bf16[256,256]{1,0:T(8,128)(2,1)S(1)}, u32[]{:S(2)}, u32[]{:S(2)}) collective-permute-start(bf16[256,256]{1,0:T(8,128)(2,1)S(1)} %get-tuple-element.161), channel_id=1, source_target_pairs={{0,4},{2,6},{4,0},{6,2},{8,12},{10,14},{12,8},{14,10},{16,20},{18,... | collective-permute-start | bytes 393224 | tf_op jit(solution)/shard_map/ppermute | solution.py:50
  87.6 1.9 %collective-permute-start.32 = (bf16[256,256]{1,0:T(8,128)(2,1)S(1)}, bf16[256,256]{1,0:T(8,128)(2,1)S(1)}, u32[]{:S(2)}, u32[]{:S(2)}) collective-permute-start(bf16[256,256]{1,0:T(8,128)(2,1)S(1)} %shard_map.97), channel_id=1, source_target_pairs={{0,8},{2,10},{4,12},{6,14},{8,0},{10,2},{12,4},{14,6},{16,24},{18,... | collective-permute-start | bytes 393224 | tf_op jit(solution)/shard_map/ppermute | solution.py:50
  90.5 2.9 %collective-permute-start.28 = (bf16[256,256]{1,0:T(8,128)(2,1)S(1)}, bf16[256,256]{1,0:T(8,128)(2,1)S(1)}, u32[]{:S(2)}, u32[]{:S(2)}) collective-permute-start(bf16[256,256]{1,0:T(8,128)(2,1)S(1)} %shard_map.95), channel_id=1, source_target_pairs={{0,24},{2,26},{4,28},{6,30},{8,16},{10,18},{12,20},{14,22},{16,8},... | collective-permute-start | bytes 393224 | tf_op jit(solution)/shard_map/ppermute | solution.py:50
  95.7 2.6 %collective-permute-done.30.refs_3_ = bf16[256,256]{1,0:T(8,128)(2,1)S(1)} collective-permute-done((bf16[256,256]{1,0:T(8,128)(2,1)S(1)}, bf16[256,256]{1,0:T(8,128)(2,1)S(1)}, u32[]{:S(2)}, u32[]{:S(2)}) %collective-permute-start.30) | collective-permute-done | bytes 131104 | tf_op jit(solution)/shard_map/ppermute | solution.py:50
  (111 shorter events, 24.1 us)
Async XLA Ops:
  1.6 4.8 %collective-permute-start = (f32[1,256]{1,0:T(1,128)S(1)}, f32[1,256]{1,0:T(1,128)S(1)}, u32[]{:S(2)}, u32[]{:S(2)}) collective-permute-start(f32[1,256]{1,0:T(1,128)S(1)} %bitcast.33), channel_id=1, source_target_pairs={{0,2},{2,0},{4,6},{6,4},{8,10},{10,8},{12,14},{14,12},{16,18},{18,... | collective-permute-start | bytes 3080 | tf_op jit(solution)/shard_map/ppermute | solution.py:50
  6.5 27.9 %collective-permute-start.9 = (bf16[512,1024]{1,0:T(8,128)(2,1)S(1)}, bf16[512,1024]{1,0:T(8,128)(2,1)S(1)}, u32[]{:S(2)}, u32[]{:S(2)}) collective-permute-start(bf16[512,1024]{1,0:T(8,128)(2,1)S(1)} %pad_maximum_fusion), channel_id=1, source_target_pairs={{0,2},{2,0},{4,6},{6,4},{8,10},{10,8},{12,14},{14,12},{16,18},{18,... | collective-permute-start | bytes 3145736 | tf_op jit(solution)/shard_map/ppermute | solution.py:50
  8.2 5.2 %collective-permute-start.3 = (bf16[272,256]{1,0:T(8,128)(2,1)S(1)}, bf16[272,256]{1,0:T(8,128)(2,1)S(1)}, u32[]{:S(2)}, u32[]{:S(2)}) collective-permute-start(bf16[272,256]{1,0:T(8,128)(2,1)S(1)} %shard_map.84.refs_0_), channel_id=1, source_target_pairs={{0,4},{2,6},{4,0},{6,2},{8,12},{10,14},{12,8},{14,10},{16,20},{18,... | collective-permute-start | bytes 417800 | tf_op jit(solution)/shard_map/ppermute | solution.py:50
  9.8 7.4 %collective-permute-start.2 = (bf16[272,256]{1,0:T(8,128)(2,1)S(1)}, bf16[272,256]{1,0:T(8,128)(2,1)S(1)}, u32[]{:S(2)}, u32[]{:S(2)}) collective-permute-start(bf16[272,256]{1,0:T(8,128)(2,1)S(1)} %shard_map.84.refs_0_), channel_id=1, source_target_pairs={{0,24},{2,26},{4,28},{6,30},{8,16},{10,18},{12,20},{14,22},{16,8},... | collective-permute-start | bytes 417800 | tf_op jit(solution)/shard_map/ppermute | solution.py:50
  13.4 10.3 %collective-permute-start.1 = (bf16[272,256]{1,0:T(8,128)(2,1)S(1)}, bf16[272,256]{1,0:T(8,128)(2,1)S(1)}, u32[]{:S(2)}, u32[]{:S(2)}) collective-permute-start(bf16[272,256]{1,0:T(8,128)(2,1)S(1)} %shard_map.84.refs_0_), channel_id=1, source_target_pairs={{0,16},{2,18},{4,20},{6,22},{8,24},{10,26},{12,28},{14,30},{16,0},... | collective-permute-start | bytes 417800 | tf_op jit(solution)/shard_map/ppermute | solution.py:50
  23.7 5.1 %collective-permute-start.4 = (bf16[272,256]{1,0:T(8,128)(2,1)S(1)}, bf16[272,256]{1,0:T(8,128)(2,1)S(1)}, u32[]{:S(2)}, u32[]{:S(2)}) collective-permute-start(bf16[272,256]{1,0:T(8,128)(2,1)S(1)} %shard_map.84.refs_0_), channel_id=1, source_target_pairs={{0,8},{2,10},{4,12},{6,14},{8,0},{10,2},{12,4},{14,6},{16,24},{18,... | collective-permute-start | bytes 417800 | tf_op jit(solution)/shard_map/ppermute | solution.py:50
  23.7 6.4 %collective-permute-start.6 = (bf16[272,256]{1,0:T(8,128)(2,1)S(1)}, bf16[272,256]{1,0:T(8,128)(2,1)S(1)}, u32[]{:S(2)}, u32[]{:S(2)}) collective-permute-start(bf16[272,256]{1,0:T(8,128)(2,1)S(1)} %collective-permute-done.1.refs_2_), channel_id=1, source_target_pairs={{0,4},{2,6},{4,0},{6,2},{8,12},{10,14},{12,8},{14,10},{16,20},{18,... | collective-permute-start | bytes 417800 | tf_op jit(solution)/shard_map/ppermute | solution.py:50
  24.2 8.6 %collective-permute-start.7 = (bf16[272,256]{1,0:T(8,128)(2,1)S(1)}, bf16[272,256]{1,0:T(8,128)(2,1)S(1)}, u32[]{:S(2)}, u32[]{:S(2)}) collective-permute-start(bf16[272,256]{1,0:T(8,128)(2,1)S(1)} %collective-permute-done.2.refs_3_), channel_id=1, source_target_pairs={{0,4},{2,6},{4,0},{6,2},{8,12},{10,14},{12,8},{14,10},{16,20},{18,... | collective-permute-start | bytes 417800 | tf_op jit(solution)/shard_map/ppermute | solution.py:50
  28.8 5.6 %collective-permute-start.5 = (bf16[272,256]{1,0:T(8,128)(2,1)S(1)}, bf16[272,256]{1,0:T(8,128)(2,1)S(1)}, u32[]{:S(2)}, u32[]{:S(2)}) collective-permute-start(bf16[272,256]{1,0:T(8,128)(2,1)S(1)} %collective-permute-done.4.refs_1_), channel_id=1, source_target_pairs={{0,4},{2,6},{4,0},{6,2},{8,12},{10,14},{12,8},{14,10},{16,20},{18,... | collective-permute-start | bytes 417800 | tf_op jit(solution)/shard_map/ppermute | solution.py:50
  29.4 6.1 %collective-permute-start.8 = (bf16[512,1024]{1,0:T(8,128)(2,1)S(1)}, bf16[512,1024]{1,0:T(8,128)(2,1)S(1)}, u32[]{:S(2)}, u32[]{:S(2)}) collective-permute-start(bf16[512,1024]{1,0:T(8,128)(2,1)S(1)} %pad_maximum_fusion.1.refs_8_.refs_0_), channel_id=1, source_target_pairs={{0,1},{1,0},{2,3},{3,2},{4,5},{5,4},{6,7},{7,6},{8,9},{9,8},{10,11... | collective-permute-start | bytes 3145736 | tf_op jit(solution)/shard_map/ppermute | solution.py:50
  34.4 5.1 %collective-permute-start.10 = (bf16[512,1024]{1,0:T(8,128)(2,1)S(1)}, bf16[512,1024]{1,0:T(8,128)(2,1)S(1)}, u32[]{:S(2)}, u32[]{:S(2)}) collective-permute-start(bf16[512,1024]{1,0:T(8,128)(2,1)S(1)} %collective-permute-done.9.refs_0_.refs_1_), channel_id=1, source_target_pairs={{0,1},{1,0},{2,3},{3,2},{4,5},{5,4},{6,7},{7,6},{8,9},{9,8},{10,11... | collective-permute-start | bytes 3145736 | tf_op jit(solution)/shard_map/ppermute | solution.py:50
  34.4 6.9 %collective-permute-start.13 = (bf16[512,128]{1,0:T(8,128)(2,1)S(1)}, bf16[512,128]{1,0:T(8,128)(2,1)S(1)}, u32[]{:S(2)}, u32[]{:S(2)}) collective-permute-start(bf16[512,128]{1,0:T(8,128)(2,1)S(1)} %get-tuple-element.180), channel_id=1, source_target_pairs={{0,2},{2,0},{4,6},{6,4},{8,10},{10,8},{12,14},{14,12},{16,18},{18,... | collective-permute-start | bytes 393224 | tf_op jit(solution)/shard_map/ppermute | solution.py:50
  38.4 6.4 %collective-permute-start.12 = (bf16[512,128]{1,0:T(8,128)(2,1)S(1)}, bf16[512,128]{1,0:T(8,128)(2,1)S(1)}, u32[]{:S(2)}, u32[]{:S(2)}) collective-permute-start(bf16[512,128]{1,0:T(8,128)(2,1)S(1)} %get-tuple-element.86), channel_id=1, source_target_pairs={{0,2},{2,0},{4,6},{6,4},{8,10},{10,8},{12,14},{14,12},{16,18},{18,... | collective-permute-start | bytes 393224 | tf_op jit(solution)/shard_map/ppermute | solution.py:50
  40.2 7.4 %collective-permute-start.11 = (bf16[512,128]{1,0:T(8,128)(2,1)S(1)}, bf16[512,128]{1,0:T(8,128)(2,1)S(1)}, u32[]{:S(2)}, u32[]{:S(2)}) collective-permute-start(bf16[512,128]{1,0:T(8,128)(2,1)S(1)} %get-tuple-element.84), channel_id=1, source_target_pairs={{0,2},{2,0},{4,6},{6,4},{8,10},{10,8},{12,14},{14,12},{16,18},{18,... | collective-permute-start | bytes 393224 | tf_op jit(solution)/shard_map/ppermute | solution.py:50
  41.3 12.4 %collective-permute-start.16 = (bf16[512,128]{1,0:T(8,128)(2,1)S(1)}, bf16[512,128]{1,0:T(8,128)(2,1)S(1)}, u32[]{:S(2)}, u32[]{:S(2)}) collective-permute-start(bf16[512,128]{1,0:T(8,128)(2,1)S(1)} %get-tuple-element.176), channel_id=1, source_target_pairs={{0,2},{2,0},{4,6},{6,4},{8,10},{10,8},{12,14},{14,12},{16,18},{18,... | collective-permute-start | bytes 393224 | tf_op jit(solution)/shard_map/ppermute | solution.py:50
  47.9 4.0 %collective-permute-start.14 = (bf16[128,128]{1,0:T(8,128)(2,1)S(1)}, bf16[128,128]{1,0:T(8,128)(2,1)S(1)}, u32[]{:S(2)}, u32[]{:S(2)}) collective-permute-start(bf16[128,128]{1,0:T(8,128)(2,1)S(1)} %get-tuple-element.91), channel_id=1, source_target_pairs={{0,4},{2,6},{4,0},{6,2},{8,12},{10,14},{12,8},{14,10},{16,20},{18,... | collective-permute-start | bytes 98312 | tf_op jit(solution)/shard_map/ppermute | solution.py:50
  48.5 5.2 %collective-permute-start.17 = (bf16[512,128]{1,0:T(8,128)(2,1)S(1)}, bf16[512,128]{1,0:T(8,128)(2,1)S(1)}, u32[]{:S(2)}, u32[]{:S(2)}) collective-permute-start(bf16[512,128]{1,0:T(8,128)(2,1)S(1)} %get-tuple-element.172), channel_id=1, source_target_pairs={{0,2},{2,0},{4,6},{6,4},{8,10},{10,8},{12,14},{14,12},{16,18},{18,... | collective-permute-start | bytes 393224 | tf_op jit(solution)/shard_map/ppermute | solution.py:50
  55.9 4.9 %collective-permute-start.18 = (bf16[128,128]{1,0:T(8,128)(2,1)S(1)}, bf16[128,128]{1,0:T(8,128)(2,1)S(1)}, u32[]{:S(2)}, u32[]{:S(2)}) collective-permute-start(bf16[128,128]{1,0:T(8,128)(2,1)S(1)} %fusion.2), channel_id=1, source_target_pairs={{0,16},{2,18},{4,20},{6,22},{8,24},{10,26},{12,28},{14,30},{16,0},... | collective-permute-start | bytes 98312 | tf_op jit(solution)/shard_map/ppermute | solution.py:50
  61.6 4.4 %collective-permute-start.19 = (bf16[128,128]{1,0:T(8,128)(2,1)S(1)}, bf16[128,128]{1,0:T(8,128)(2,1)S(1)}, u32[]{:S(2)}, u32[]{:S(2)}) collective-permute-start(bf16[128,128]{1,0:T(8,128)(2,1)S(1)} %get-tuple-element.110), channel_id=1, source_target_pairs={{0,4},{2,6},{4,0},{6,2},{8,12},{10,14},{12,8},{14,10},{16,20},{18,... | collective-permute-start | bytes 98312 | tf_op jit(solution)/shard_map/ppermute | solution.py:50
  62.9 6.4 %collective-permute-start.21 = (bf16[512,128]{1,0:T(8,128)(2,1)S(1)}, bf16[512,128]{1,0:T(8,128)(2,1)S(1)}, u32[]{:S(2)}, u32[]{:S(2)}) collective-permute-start(bf16[512,128]{1,0:T(8,128)(2,1)S(1)} %get-tuple-element.168), channel_id=1, source_target_pairs={{0,2},{2,0},{4,6},{6,4},{8,10},{10,8},{12,14},{14,12},{16,18},{18,... | collective-permute-start | bytes 393224 | tf_op jit(solution)/shard_map/ppermute | solution.py:50
  66.0 4.5 %collective-permute-start.20 = (bf16[128,128]{1,0:T(8,128)(2,1)S(1)}, bf16[128,128]{1,0:T(8,128)(2,1)S(1)}, u32[]{:S(2)}, u32[]{:S(2)}) collective-permute-start(bf16[128,128]{1,0:T(8,128)(2,1)S(1)} %fusion.8), channel_id=1, source_target_pairs={{0,8},{2,10},{4,12},{6,14},{8,0},{10,2},{12,4},{14,6},{16,24},{18,... | collective-permute-start | bytes 98312 | tf_op jit(solution)/shard_map/ppermute | solution.py:50
  69.4 6.4 %collective-permute-start.23 = (bf16[1024,128]{1,0:T(8,128)(2,1)S(1)}, bf16[1024,128]{1,0:T(8,128)(2,1)S(1)}, u32[]{:S(2)}, u32[]{:S(2)}) collective-permute-start(bf16[1024,128]{1,0:T(8,128)(2,1)S(1)} %get-tuple-element.124), channel_id=1, source_target_pairs={{0,2},{2,0},{4,6},{6,4},{8,10},{10,8},{12,14},{14,12},{16,18},{18,... | collective-permute-start | bytes 786440 | tf_op jit(solution)/shard_map/ppermute | solution.py:50
  70.5 4.9 %collective-permute-start.22 = (bf16[128,128]{1,0:T(8,128)(2,1)S(1)}, bf16[128,128]{1,0:T(8,128)(2,1)S(1)}, u32[]{:S(2)}, u32[]{:S(2)}) collective-permute-start(bf16[128,128]{1,0:T(8,128)(2,1)S(1)} %fusion.6), channel_id=1, source_target_pairs={{0,16},{2,18},{4,20},{6,22},{8,24},{10,26},{12,28},{14,30},{16,0},... | collective-permute-start | bytes 98312 | tf_op jit(solution)/shard_map/ppermute | solution.py:50
  75.7 4.3 %collective-permute-start.24 = (bf16[128,128]{1,0:T(8,128)(2,1)S(1)}, bf16[128,128]{1,0:T(8,128)(2,1)S(1)}, u32[]{:S(2)}, u32[]{:S(2)}) collective-permute-start(bf16[128,128]{1,0:T(8,128)(2,1)S(1)} %fusion.5.after_ref), channel_id=1, source_target_pairs={{0,2},{2,0},{4,6},{6,4},{8,10},{10,8},{12,14},{14,12},{16,18},{18,... | collective-permute-start | bytes 98312 | tf_op jit(solution)/shard_map/ppermute | solution.py:50
  81.4 12.0 %collective-permute-start.25 = (bf16[3,512,128]{2,1,0:T(8,128)(2,1)S(1)}, bf16[3,512,128]{2,1,0:T(8,128)(2,1)S(1)}, u32[]{:S(2)}, u32[]{:S(2)}) collective-permute-start(bf16[3,512,128]{2,1,0:T(8,128)(2,1)S(1)} %pad_maximum_fusion.2), channel_id=1, source_target_pairs={{0,2},{2,0},{4,6},{6,4},{8,10},{10,8},{12,14},{14,12},{16,18},{18,... | collective-permute-start | bytes 1179656 | tf_op jit(solution)/shard_map/ppermute | solution.py:50
  82.5 5.0 %collective-permute-start.31 = (bf16[256,256]{1,0:T(8,128)(2,1)S(1)}, bf16[256,256]{1,0:T(8,128)(2,1)S(1)}, u32[]{:S(2)}, u32[]{:S(2)}) collective-permute-start(bf16[256,256]{1,0:T(8,128)(2,1)S(1)} %get-tuple-element.158), channel_id=1, source_target_pairs={{0,4},{2,6},{4,0},{6,2},{8,12},{10,14},{12,8},{14,10},{16,20},{18,... | collective-permute-start | bytes 393224 | tf_op jit(solution)/shard_map/ppermute | solution.py:50
  83.4 6.1 %collective-permute-start.29 = (bf16[256,256]{1,0:T(8,128)(2,1)S(1)}, bf16[256,256]{1,0:T(8,128)(2,1)S(1)}, u32[]{:S(2)}, u32[]{:S(2)}) collective-permute-start(bf16[256,256]{1,0:T(8,128)(2,1)S(1)} %get-tuple-element.159), channel_id=1, source_target_pairs={{0,4},{2,6},{4,0},{6,2},{8,12},{10,14},{12,8},{14,10},{16,20},{18,... | collective-permute-start | bytes 393224 | tf_op jit(solution)/shard_map/ppermute | solution.py:50
  84.6 5.9 %collective-permute-start.27 = (bf16[256,256]{1,0:T(8,128)(2,1)S(1)}, bf16[256,256]{1,0:T(8,128)(2,1)S(1)}, u32[]{:S(2)}, u32[]{:S(2)}) collective-permute-start(bf16[256,256]{1,0:T(8,128)(2,1)S(1)} %get-tuple-element.160), channel_id=1, source_target_pairs={{0,4},{2,6},{4,0},{6,2},{8,12},{10,14},{12,8},{14,10},{16,20},{18,... | collective-permute-start | bytes 393224 | tf_op jit(solution)/shard_map/ppermute | solution.py:50
  85.4 10.2 %collective-permute-start.26 = (bf16[256,256]{1,0:T(8,128)(2,1)S(1)}, bf16[256,256]{1,0:T(8,128)(2,1)S(1)}, u32[]{:S(2)}, u32[]{:S(2)}) collective-permute-start(bf16[256,256]{1,0:T(8,128)(2,1)S(1)} %get-tuple-element.161), channel_id=1, source_target_pairs={{0,4},{2,6},{4,0},{6,2},{8,12},{10,14},{12,8},{14,10},{16,20},{18,... | collective-permute-start | bytes 393224 | tf_op jit(solution)/shard_map/ppermute | solution.py:50
  87.6 8.1 %collective-permute-start.32 = (bf16[256,256]{1,0:T(8,128)(2,1)S(1)}, bf16[256,256]{1,0:T(8,128)(2,1)S(1)}, u32[]{:S(2)}, u32[]{:S(2)}) collective-permute-start(bf16[256,256]{1,0:T(8,128)(2,1)S(1)} %shard_map.97), channel_id=1, source_target_pairs={{0,8},{2,10},{4,12},{6,14},{8,0},{10,2},{12,4},{14,6},{16,24},{18,... | collective-permute-start | bytes 393224 | tf_op jit(solution)/shard_map/ppermute | solution.py:50
  89.6 8.7 %collective-permute-start.30 = (bf16[256,256]{1,0:T(8,128)(2,1)S(1)}, bf16[256,256]{1,0:T(8,128)(2,1)S(1)}, u32[]{:S(2)}, u32[]{:S(2)}) collective-permute-start(bf16[256,256]{1,0:T(8,128)(2,1)S(1)} %shard_map.96), channel_id=1, source_target_pairs={{0,16},{2,18},{4,20},{6,22},{8,24},{10,26},{12,28},{14,30},{16,0},... | collective-permute-start | bytes 393224 | tf_op jit(solution)/shard_map/ppermute | solution.py:50
  90.5 7.8 %collective-permute-start.28 = (bf16[256,256]{1,0:T(8,128)(2,1)S(1)}, bf16[256,256]{1,0:T(8,128)(2,1)S(1)}, u32[]{:S(2)}, u32[]{:S(2)}) collective-permute-start(bf16[256,256]{1,0:T(8,128)(2,1)S(1)} %shard_map.95), channel_id=1, source_target_pairs={{0,24},{2,26},{4,28},{6,30},{8,16},{10,18},{12,20},{14,22},{16,8},... | collective-permute-start | bytes 393224 | tf_op jit(solution)/shard_map/ppermute | solution.py:50
  (17 other events, 215.6 us)

commit v3 on v2

--- a/solution.py
+++ b/solution.py
@@ -293,12 +293,13 @@
     odd = [swap(slab, "seq", 2)] + [None] * (far - 1)
     for i in range(2, far):
         even[i] = swap(slab, "seq", 4 * i)
-    even[2:], odd[0], slab_late = lax.optimization_barrier((even[2:], odd[0], slab))
+    if far > 1:
+        even[1] = swap(slab, "seq", 4)
+        held, odd[0] = lax.optimization_barrier((even[1], odd[0]))
+        odd[1] = swap(held, "seq", 2)
+    even[2:], odd[:2] = lax.optimization_barrier((even[2:], odd[:2]))
     for i in range(2, far):
         odd[i] = swap(even[i], "seq", 2)
-    if far > 1:
-        even[1] = swap(slab_late, "seq", 4)
-        odd[1] = swap(even[1], "seq", 2)
     slab_list = even + odd
     own_late, _ = lax.optimization_barrier((own_half, even[-1]))
     own_pieces = [own_half] + [swap(own_late, "head", k) for k in range(1, heads)]
@@ -377,11 +378,11 @@
             4 * cost,
         )
 
-    prior, (pieces, (q, up)) = scan(
+    prior, (_, (pieces, (q, up))) = scan(
         total,
         total16,
         False,
-        [lambda _: parked, lambda late: [joined(*a, late) for a in early]],
+        [lambda _: (), lambda late: (parked, [joined(*a, late) for a in early])],
     )
     mixed, local_prior = intra()
     out, gm, gtotal, gtotal16 = call(
@@ -432,13 +433,13 @@
 
     arrived = []
     for i in reversed(range(1, far)):
-        (joined,) = call(
-            functools.partial(join_kernel, i),
-            [shape((columns, rows), BF16)],
-            [keep_parts, swap(send_parts[i], "seq", 2)],
-            0,
+        got = swap(send_parts[i], "seq", 2)
+        if arrived:
+            got, _ = lax.optimization_barrier((got, joint))
+        (joint,) = call(
+            functools.partial(join_kernel, i), [shape((columns, rows), BF16)], [keep_parts, got], 0
         )
-        arrived.append(swap(joined, "seq", 4 * i))
+        arrived.append(swap(joint, "seq", 4 * i))
     terms = [keep_parts, swap(send_parts[0], "seq", 2)] + arrived
     def token_half(flag):
         return jnp.stack([pick(flag, a[:tokens], a[tokens:]) for a in (out, gq, gk)])

time: 99.3 us -> 96.6 us (0.973)
  waiting for transfers between devices: 38.8 us -> 33.9 us
  starting transfers between devices: 40.7 us -> 42.8 us
    ppermute x33, waiting for transfers between devices: 38.8 us -> 33.9 us  [swap(): return lax.ppermute(array, axis, [(i, i ^ distance) for i in range(count)])]
    ppermute x33, starting transfers between devices: 40.7 us -> 42.8 us  [swap(): return lax.ppermute(array, axis, [(i, i ^ distance) for i in range(count)])]
  transfers between devices with their start and end apart: 33 -> 33, of which waited for: 17 -> 15; matrix products, arithmetic and copies ran while one was open for 5% -> 5% of each run, Pallas kernels for 10% -> 10%
where the time goes in v3:
time: 96.6 us; the launch traced here: 96.3 us
  starting transfers between devices  42.8 us (44%)
  waiting for transfers between devices  33.9 us (35%)
  Pallas kernels  12.8 us (13%)
  other arithmetic  5.65 us (6%)
  between operations  1.07 us (1%)
    ppermute x33, starting transfers between devices, swap(): return lax.ppermute(array, axis, [(i, i ^ distance) for i in range(count)])  42.8 us
    ppermute x33, waiting for transfers between devices, swap(): return lax.ppermute(array, axis, [(i, i ^ distance) for i in range(count)])  33.9 us
    pallas_call x14, Pallas kernels, call(): pl.pallas_call(kernel, out_shape=outs, in_specs=specs or vmem_specs(len(a...  10.8 us
    concatenate x3, other arithmetic, per_device(): jnp.concatenate([pick(side, mine[i], theirs[i]), pick(side, theirs[i], mi...  2.2 us
    pallas_call x1, Pallas kernels, park(): pl.pallas_call(functools.partial(park_kernel, n), out_shape=[pltpu.HBM(a....  2.02 us
  transfers between devices with their start and end apart: 33, of which 15 were waited for; matrix products, arithmetic and copies ran while one was open for 5% of the time, Pallas kernels for 10%

profile of v3, /device:TPU:0, one launch (start us, length us, event | category | flops | bytes accessed | tf_op | source)
XLA Modules:
  0.0 96.3 jit_solution(16976697250330607416)
XLA Ops:
  1.6 3.0 %collective-permute-start = (f32[1,256]{1,0:T(1,128)S(1)}, f32[1,256]{1,0:T(1,128)S(1)}, u32[]{:S(2)}, u32[]{:S(2)}) collective-permute-start(f32[1,256]{1,0:T(1,128)S(1)} %bitcast.33), channel_id=1, source_target_pairs={{0,2},{2,0},{4,6},{6,4},{8,10},{10,8},{12,14},{14,12},{16,18},{18,... | collective-permute-start | bytes 3080 | tf_op jit(solution)/shard_map/ppermute | solution.py:50
  4.6 1.7 %broadcast_select_fusion.3 = (bf16[512,256]{1,0:T(8,128)(2,1)S(1)}, bf16[512,256]{1,0:T(8,128)(2,1)S(1)}, bf16[512,256]{1,0:T(8,128)(2,1)S(1)}, bf16[512,256]{1,...) fusion(pred[]{:T(512)S(6)} %eq.16, ...), kind=kLoop, calls=%fused_computation.14 | loop fusion | flops 1048576 | bytes 4194306 | tf_op jit(solution)/shard_map/jit(_where)/select_n | solution.py:267
  6.5 1.7 %collective-permute-start.9 = (bf16[512,1024]{1,0:T(8,128)(2,1)S(1)}, bf16[512,1024]{1,0:T(8,128)(2,1)S(1)}, u32[]{:S(2)}, u32[]{:S(2)}) collective-permute-start(bf16[512,1024]{1,0:T(8,128)(2,1)S(1)} %pad_maximum_fusion), channel_id=1, source_target_pairs={{0,2},{2,0},{4,6},{6,4},{8,10},{10,8},{12,14},{14,12},{16,18},{18,... | collective-permute-start | bytes 3145736 | tf_op jit(solution)/shard_map/ppermute | solution.py:50
  8.2 1.6 %collective-permute-start.4 = (bf16[272,256]{1,0:T(8,128)(2,1)S(1)}, bf16[272,256]{1,0:T(8,128)(2,1)S(1)}, u32[]{:S(2)}, u32[]{:S(2)}) collective-permute-start(bf16[272,256]{1,0:T(8,128)(2,1)S(1)} %shard_map.84.refs_0_), channel_id=1, source_target_pairs={{0,4},{2,6},{4,0},{6,2},{8,12},{10,14},{12,8},{14,10},{16,20},{18,... | collective-permute-start | bytes 417800 | tf_op jit(solution)/shard_map/ppermute | solution.py:50
  9.8 1.6 %collective-permute-start.1 = (bf16[272,256]{1,0:T(8,128)(2,1)S(1)}, bf16[272,256]{1,0:T(8,128)(2,1)S(1)}, u32[]{:S(2)}, u32[]{:S(2)}) collective-permute-start(bf16[272,256]{1,0:T(8,128)(2,1)S(1)} %shard_map.84.refs_0_), channel_id=1, source_target_pairs={{0,8},{2,10},{4,12},{6,14},{8,0},{10,2},{12,4},{14,6},{16,24},{18,... | collective-permute-start | bytes 417800 | tf_op jit(solution)/shard_map/ppermute | solution.py:50
  11.4 2.5 %collective-permute-start.3 = (bf16[272,256]{1,0:T(8,128)(2,1)S(1)}, bf16[272,256]{1,0:T(8,128)(2,1)S(1)}, u32[]{:S(2)}, u32[]{:S(2)}) collective-permute-start(bf16[272,256]{1,0:T(8,128)(2,1)S(1)} %shard_map.84.refs_0_), channel_id=1, source_target_pairs={{0,24},{2,26},{4,28},{6,30},{8,16},{10,18},{12,20},{14,22},{16,8},... | collective-permute-start | bytes 417800 | tf_op jit(solution)/shard_map/ppermute | solution.py:50
  14.0 2.7 %collective-permute-done.1.refs_1_ = bf16[272,256]{1,0:T(8,128)(2,1)S(1)} collective-permute-done((bf16[272,256]{1,0:T(8,128)(2,1)S(1)}, bf16[272,256]{1,0:T(8,128)(2,1)S(1)}, u32[]{:S(2)}, u32[]{:S(2)}) %collective-permute-start.1) | collective-permute-done | bytes 139296 | tf_op jit(solution)/shard_map/ppermute | solution.py:50
  17.2 3.1 %collective-permute-done.3.refs_3_ = bf16[272,256]{1,0:T(8,128)(2,1)S(1)} collective-permute-done((bf16[272,256]{1,0:T(8,128)(2,1)S(1)}, bf16[272,256]{1,0:T(8,128)(2,1)S(1)}, u32[]{:S(2)}, u32[]{:S(2)}) %collective-permute-start.3) | collective-permute-done | bytes 139296 | tf_op jit(solution)/shard_map/ppermute | solution.py:50
  20.3 4.5 %collective-permute-done.2.refs_2_ = bf16[272,256]{1,0:T(8,128)(2,1)S(1)} collective-permute-done((bf16[272,256]{1,0:T(8,128)(2,1)S(1)}, bf16[272,256]{1,0:T(8,128)(2,1)S(1)}, u32[]{:S(2)}, u32[]{:S(2)}) %collective-permute-start.2) | collective-permute-done | bytes 139296 | tf_op jit(solution)/shard_map/ppermute | solution.py:50
  25.4 1.5 %collective-permute-start.7 = (bf16[272,256]{1,0:T(8,128)(2,1)S(1)}, bf16[272,256]{1,0:T(8,128)(2,1)S(1)}, u32[]{:S(2)}, u32[]{:S(2)}) collective-permute-start(bf16[272,256]{1,0:T(8,128)(2,1)S(1)} %collective-permute-done.3.refs_3_), channel_id=1, source_target_pairs={{0,4},{2,6},{4,0},{6,2},{8,12},{10,14},{12,8},{14,10},{16,20},{18,... | collective-permute-start | bytes 417800 | tf_op jit(solution)/shard_map/ppermute | solution.py:50
  27.1 3.1 %collective-permute-done.6.refs_6_ = bf16[272,256]{1,0:T(8,128)(2,1)S(1)} collective-permute-done((bf16[272,256]{1,0:T(8,128)(2,1)S(1)}, bf16[272,256]{1,0:T(8,128)(2,1)S(1)}, u32[]{:S(2)}, u32[]{:S(2)}) %collective-permute-start.6) | collective-permute-done | bytes 139296 | tf_op jit(solution)/shard_map/ppermute | solution.py:50
  30.3 1.5 %collective-permute-done.7.refs_7_ = bf16[272,256]{1,0:T(8,128)(2,1)S(1)} collective-permute-done((bf16[272,256]{1,0:T(8,128)(2,1)S(1)}, bf16[272,256]{1,0:T(8,128)(2,1)S(1)}, u32[]{:S(2)}, u32[]{:S(2)}) %collective-permute-start.7) | collective-permute-done | bytes 139296 | tf_op jit(solution)/shard_map/ppermute | solution.py:50
  33.0 2.8 %shard_map.85 = (bf16[2048,256]{1,0:T(8,128)(2,1)S(1)}, f32[512,128]{1,0:T(8,128)S(1)}, bf16[512,128]{1,0:T(8,128)(2,1)S(1)}) custom-call(bf16[272,256]{1,0:T(8,128)(2,1)} %copy-done.5, bf16[272,256]{1,0:T(8,128)(2,1)} %copy-done.10, bf16[272,256]{1,0:T(8,128)(2,1)} %copy-done.12, bf16[272,256]{1,0:T(8,128)(2,1)} %copy-done.11, bf16[272,256]{1,0:T(8,128)(2,1)} %copy-done.9, ...), custom_call_target="tpu_custom_call" | custom-call | flops 536870912 | bytes 4653056 | tf_op jit(solution)/shard_map/pallas_call | solution.py:135
  39.8 2.4 %collective-permute-done.12.got_got_ref = bf16[512,128]{1,0:T(8,128)(2,1)S(1)} collective-permute-done((bf16[512,128]{1,0:T(8,128)(2,1)S(1)}, bf16[512,128]{1,0:T(8,128)(2,1)S(1)}, u32[]{:S(2)}, u32[]{:S(2)}) %collective-permute-start.12) | collective-permute-done | bytes 131104 | tf_op jit(solution)/shard_map/ppermute | solution.py:50
  42.2 2.8 %collective-permute-done.11.own_got_ref = bf16[512,128]{1,0:T(8,128)(2,1)S(1)} collective-permute-done((bf16[512,128]{1,0:T(8,128)(2,1)S(1)}, bf16[512,128]{1,0:T(8,128)(2,1)S(1)}, u32[]{:S(2)}, u32[]{:S(2)}) %collective-permute-start.11) | collective-permute-done | bytes 131104 | tf_op jit(solution)/shard_map/ppermute | solution.py:50
  46.1 1.3 %collective-permute-start.17 = (bf16[512,128]{1,0:T(8,128)(2,1)S(1)}, bf16[512,128]{1,0:T(8,128)(2,1)S(1)}, u32[]{:S(2)}, u32[]{:S(2)}) collective-permute-start(bf16[512,128]{1,0:T(8,128)(2,1)S(1)} %get-tuple-element.178), channel_id=1, source_target_pairs={{0,2},{2,0},{4,6},{6,4},{8,10},{10,8},{12,14},{14,12},{16,18},{18,... | collective-permute-start | bytes 393224 | tf_op jit(solution)/shard_map/ppermute | solution.py:50
  47.4 2.0 %shard_map.88 = (bf16[512,1024]{1,0:T(8,128)(2,1)}, bf16[512,1024]{1,0:T(8,128)(2,1)}, bf16[512,1024]{1,0:T(8,128)(2,1)}, bf16[512,1024]{1,0:T(8,128)(2,1)}) custom-call(bf16[512,1024]{1,0:T(8,128)(2,1)S(1)} %pad_maximum_fusion.1.refs_8_.refs_0_, bf16[512,1024]{1,0:T(8,128)(2,1)S(1)} %collective-permute-done.9.refs_0_.refs_1_, ...), custom_call_target="tpu_custom_call" | custom-call | tf_op jit(solution)/shard_map/pallas_call | solution.py:118
  49.5 1.6 %collective-permute-start.15 = (bf16[128,128]{1,0:T(8,128)(2,1)S(1)}, bf16[128,128]{1,0:T(8,128)(2,1)S(1)}, u32[]{:S(2)}, u32[]{:S(2)}) collective-permute-start(bf16[128,128]{1,0:T(8,128)(2,1)S(1)} %fusion.7), channel_id=1, source_target_pairs={{0,8},{2,10},{4,12},{6,14},{8,0},{10,2},{12,4},{14,6},{16,24},{18,... | collective-permute-start | bytes 98312 | tf_op jit(solution)/shard_map/ppermute | solution.py:50
  51.2 2.2 %collective-permute-done.15 = bf16[128,128]{1,0:T(8,128)(2,1)S(1)} collective-permute-done((bf16[128,128]{1,0:T(8,128)(2,1)S(1)}, bf16[128,128]{1,0:T(8,128)(2,1)S(1)}, u32[]{:S(2)}, u32[]{:S(2)}) %collective-permute-start.15) | collective-permute-done | bytes 32800 | tf_op jit(solution)/shard_map/ppermute | solution.py:50
  53.5 2.8 %collective-permute-start.18 = (bf16[128,128]{1,0:T(8,128)(2,1)S(1)}, bf16[128,128]{1,0:T(8,128)(2,1)S(1)}, u32[]{:S(2)}, u32[]{:S(2)}) collective-permute-start(bf16[128,128]{1,0:T(8,128)(2,1)S(1)} %fusion.2), channel_id=1, source_target_pairs={{0,16},{2,18},{4,20},{6,22},{8,24},{10,26},{12,28},{14,30},{16,0},... | collective-permute-start | bytes 98312 | tf_op jit(solution)/shard_map/ppermute | solution.py:50
  56.2 1.4 %shard_map.89 = (f32[1024,128]{1,0:T(8,128)S(1)}, bf16[8,128,128]{2,1,0:T(8,128)(2,1)S(1)}) custom-call(bf16[1024,128]{1,0:T(8,128)(2,1)S(1)} %get-tuple-element.108.q_ref, bf16[1024,128]{1,0:T(8,128)(2,1)S(1)} %pad_maximum_fusion.3.k_ref, bf16[1024,128]{1,0:T(8,128)(2,1)S(1)} %get-tuple-element.97.refs_4_.v_ref), custom_call_target="tpu_custom_call" | custom-call | flops 134217728 | bytes 1572864 | tf_op jit(solution)/shard_map/pallas_call | solution.py:135
  61.4 1.9 %shard_map.91 = (bf16[1024,128]{1,0:T(8,128)(2,1)S(1)}, f32[1024,128]{1,0:T(8,128)S(1)}, f32[1024,128]{1,0:T(8,128)S(1)}, bf16[1024,128]{1,0:T(8,128)(2,1)S(1)}) custom-call(bf16[1024,128]{1,0:T(8,128)(2,1)S(1)} %get-tuple-element.108.q_ref, bf16[1024,128]{1,0:T(8,128)(2,1)S(1)} %pad_maximum_fusion.3.k_ref, ...), custom_call_target="tpu_custom_call" | custom-call | flops 301989888 | bytes 2949120 | tf_op jit(solution)/shard_map/pallas_call | solution.py:135
  63.4 1.4 %collective-permute-start.20 = (bf16[128,128]{1,0:T(8,128)(2,1)S(1)}, bf16[128,128]{1,0:T(8,128)(2,1)S(1)}, u32[]{:S(2)}, u32[]{:S(2)}) collective-permute-start(bf16[128,128]{1,0:T(8,128)(2,1)S(1)} %fusion.8), channel_id=1, source_target_pairs={{0,8},{2,10},{4,12},{6,14},{8,0},{10,2},{12,4},{14,6},{16,24},{18,... | collective-permute-start | bytes 98312 | tf_op jit(solution)/shard_map/ppermute | solution.py:50
  64.8 2.0 %collective-permute-done.21 = bf16[512,128]{1,0:T(8,128)(2,1)S(1)} collective-permute-done((bf16[512,128]{1,0:T(8,128)(2,1)S(1)}, bf16[512,128]{1,0:T(8,128)(2,1)S(1)}, u32[]{:S(2)}, u32[]{:S(2)}) %collective-permute-start.21) | collective-permute-done | bytes 131104 | tf_op jit(solution)/shard_map/ppermute | solution.py:50
  67.9 2.6 %collective-permute-start.22 = (bf16[128,128]{1,0:T(8,128)(2,1)S(1)}, bf16[128,128]{1,0:T(8,128)(2,1)S(1)}, u32[]{:S(2)}, u32[]{:S(2)}) collective-permute-start(bf16[128,128]{1,0:T(8,128)(2,1)S(1)} %fusion.6), channel_id=1, source_target_pairs={{0,16},{2,18},{4,20},{6,22},{8,24},{10,26},{12,28},{14,30},{16,0},... | collective-permute-start | bytes 98312 | tf_op jit(solution)/shard_map/ppermute | solution.py:50
  70.5 2.3 %collective-permute-done.22 = bf16[128,128]{1,0:T(8,128)(2,1)S(1)} collective-permute-done((bf16[128,128]{1,0:T(8,128)(2,1)S(1)}, bf16[128,128]{1,0:T(8,128)(2,1)S(1)}, u32[]{:S(2)}, u32[]{:S(2)}) %collective-permute-start.22) | collective-permute-done | bytes 32800 | tf_op jit(solution)/shard_map/ppermute | solution.py:50
  74.2 3.3 %collective-permute-done.24.after_got_ref = bf16[128,128]{1,0:T(8,128)(2,1)S(1)} collective-permute-done((bf16[128,128]{1,0:T(8,128)(2,1)S(1)}, bf16[128,128]{1,0:T(8,128)(2,1)S(1)}, u32[]{:S(2)}, u32[]{:S(2)}) %collective-permute-start.24) | collective-permute-done | bytes 32800 | tf_op jit(solution)/shard_map/ppermute | solution.py:50
  80.9 1.2 %collective-permute-start.29 = (bf16[256,256]{1,0:T(8,128)(2,1)S(1)}, bf16[256,256]{1,0:T(8,128)(2,1)S(1)}, u32[]{:S(2)}, u32[]{:S(2)}) collective-permute-start(bf16[256,256]{1,0:T(8,128)(2,1)S(1)} %get-tuple-element.165), channel_id=1, source_target_pairs={{0,4},{2,6},{4,0},{6,2},{8,12},{10,14},{12,8},{14,10},{16,20},{18,... | collective-permute-start | bytes 393224 | tf_op jit(solution)/shard_map/ppermute | solution.py:50
  82.9 1.2 %collective-permute-start.26 = (bf16[256,256]{1,0:T(8,128)(2,1)S(1)}, bf16[256,256]{1,0:T(8,128)(2,1)S(1)}, u32[]{:S(2)}, u32[]{:S(2)}) collective-permute-start(bf16[256,256]{1,0:T(8,128)(2,1)S(1)} %get-tuple-element.167), channel_id=1, source_target_pairs={{0,4},{2,6},{4,0},{6,2},{8,12},{10,14},{12,8},{14,10},{16,20},{18,... | collective-permute-start | bytes 393224 | tf_op jit(solution)/shard_map/ppermute | solution.py:50
  85.1 3.3 %collective-permute-start.28 = (bf16[256,256]{1,0:T(8,128)(2,1)S(1)}, bf16[256,256]{1,0:T(8,128)(2,1)S(1)}, u32[]{:S(2)}, u32[]{:S(2)}) collective-permute-start(bf16[256,256]{1,0:T(8,128)(2,1)S(1)} %shard_map.95), channel_id=1, source_target_pairs={{0,24},{2,26},{4,28},{6,30},{8,16},{10,18},{12,20},{14,22},{16,8},... | collective-permute-start | bytes 393224 | tf_op jit(solution)/shard_map/ppermute | solution.py:50
  89.1 1.4 %collective-permute-start.32 = (bf16[256,256]{1,0:T(8,128)(2,1)S(1)}, bf16[256,256]{1,0:T(8,128)(2,1)S(1)}, u32[]{:S(2)}, u32[]{:S(2)}) collective-permute-start(bf16[256,256]{1,0:T(8,128)(2,1)S(1)} %shard_map.97), channel_id=1, source_target_pairs={{0,8},{2,10},{4,12},{6,14},{8,0},{10,2},{12,4},{14,6},{16,24},{18,... | collective-permute-start | bytes 393224 | tf_op jit(solution)/shard_map/ppermute | solution.py:50
  92.7 2.7 %collective-permute-done.32.refs_4_ = bf16[256,256]{1,0:T(8,128)(2,1)S(1)} collective-permute-done((bf16[256,256]{1,0:T(8,128)(2,1)S(1)}, bf16[256,256]{1,0:T(8,128)(2,1)S(1)}, u32[]{:S(2)}, u32[]{:S(2)}) %collective-permute-start.32) | collective-permute-done | bytes 131104 | tf_op jit(solution)/shard_map/ppermute | solution.py:50
  (111 shorter events, 24.2 us)
Async XLA Ops:
  1.6 4.8 %collective-permute-start = (f32[1,256]{1,0:T(1,128)S(1)}, f32[1,256]{1,0:T(1,128)S(1)}, u32[]{:S(2)}, u32[]{:S(2)}) collective-permute-start(f32[1,256]{1,0:T(1,128)S(1)} %bitcast.33), channel_id=1, source_target_pairs={{0,2},{2,0},{4,6},{6,4},{8,10},{10,8},{12,14},{14,12},{16,18},{18,... | collective-permute-start | bytes 3080 | tf_op jit(solution)/shard_map/ppermute | solution.py:50
  6.5 25.3 %collective-permute-start.9 = (bf16[512,1024]{1,0:T(8,128)(2,1)S(1)}, bf16[512,1024]{1,0:T(8,128)(2,1)S(1)}, u32[]{:S(2)}, u32[]{:S(2)}) collective-permute-start(bf16[512,1024]{1,0:T(8,128)(2,1)S(1)} %pad_maximum_fusion), channel_id=1, source_target_pairs={{0,2},{2,0},{4,6},{6,4},{8,10},{10,8},{12,14},{14,12},{16,18},{18,... | collective-permute-start | bytes 3145736 | tf_op jit(solution)/shard_map/ppermute | solution.py:50
  8.2 5.8 %collective-permute-start.4 = (bf16[272,256]{1,0:T(8,128)(2,1)S(1)}, bf16[272,256]{1,0:T(8,128)(2,1)S(1)}, u32[]{:S(2)}, u32[]{:S(2)}) collective-permute-start(bf16[272,256]{1,0:T(8,128)(2,1)S(1)} %shard_map.84.refs_0_), channel_id=1, source_target_pairs={{0,4},{2,6},{4,0},{6,2},{8,12},{10,14},{12,8},{14,10},{16,20},{18,... | collective-permute-start | bytes 417800 | tf_op jit(solution)/shard_map/ppermute | solution.py:50
  9.8 6.8 %collective-permute-start.1 = (bf16[272,256]{1,0:T(8,128)(2,1)S(1)}, bf16[272,256]{1,0:T(8,128)(2,1)S(1)}, u32[]{:S(2)}, u32[]{:S(2)}) collective-permute-start(bf16[272,256]{1,0:T(8,128)(2,1)S(1)} %shard_map.84.refs_0_), channel_id=1, source_target_pairs={{0,8},{2,10},{4,12},{6,14},{8,0},{10,2},{12,4},{14,6},{16,24},{18,... | collective-permute-start | bytes 417800 | tf_op jit(solution)/shard_map/ppermute | solution.py:50
  11.4 8.9 %collective-permute-start.3 = (bf16[272,256]{1,0:T(8,128)(2,1)S(1)}, bf16[272,256]{1,0:T(8,128)(2,1)S(1)}, u32[]{:S(2)}, u32[]{:S(2)}) collective-permute-start(bf16[272,256]{1,0:T(8,128)(2,1)S(1)} %shard_map.84.refs_0_), channel_id=1, source_target_pairs={{0,24},{2,26},{4,28},{6,30},{8,16},{10,18},{12,20},{14,22},{16,8},... | collective-permute-start | bytes 417800 | tf_op jit(solution)/shard_map/ppermute | solution.py:50
  13.9 11.0 %collective-permute-start.2 = (bf16[272,256]{1,0:T(8,128)(2,1)S(1)}, bf16[272,256]{1,0:T(8,128)(2,1)S(1)}, u32[]{:S(2)}, u32[]{:S(2)}) collective-permute-start(bf16[272,256]{1,0:T(8,128)(2,1)S(1)} %shard_map.84.refs_0_), channel_id=1, source_target_pairs={{0,16},{2,18},{4,20},{6,22},{8,24},{10,26},{12,28},{14,30},{16,0},... | collective-permute-start | bytes 417800 | tf_op jit(solution)/shard_map/ppermute | solution.py:50
  16.7 8.2 %collective-permute-start.5 = (bf16[272,256]{1,0:T(8,128)(2,1)S(1)}, bf16[272,256]{1,0:T(8,128)(2,1)S(1)}, u32[]{:S(2)}, u32[]{:S(2)}) collective-permute-start(bf16[272,256]{1,0:T(8,128)(2,1)S(1)} %collective-permute-done.1.refs_1_), channel_id=1, source_target_pairs={{0,4},{2,6},{4,0},{6,2},{8,12},{10,14},{12,8},{14,10},{16,20},{18,... | collective-permute-start | bytes 417800 | tf_op jit(solution)/shard_map/ppermute | solution.py:50
  24.8 5.4 %collective-permute-start.6 = (bf16[272,256]{1,0:T(8,128)(2,1)S(1)}, bf16[272,256]{1,0:T(8,128)(2,1)S(1)}, u32[]{:S(2)}, u32[]{:S(2)}) collective-permute-start(bf16[272,256]{1,0:T(8,128)(2,1)S(1)} %collective-permute-done.2.refs_2_), channel_id=1, source_target_pairs={{0,4},{2,6},{4,0},{6,2},{8,12},{10,14},{12,8},{14,10},{16,20},{18,... | collective-permute-start | bytes 417800 | tf_op jit(solution)/shard_map/ppermute | solution.py:50
  25.4 6.3 %collective-permute-start.7 = (bf16[272,256]{1,0:T(8,128)(2,1)S(1)}, bf16[272,256]{1,0:T(8,128)(2,1)S(1)}, u32[]{:S(2)}, u32[]{:S(2)}) collective-permute-start(bf16[272,256]{1,0:T(8,128)(2,1)S(1)} %collective-permute-done.3.refs_3_), channel_id=1, source_target_pairs={{0,4},{2,6},{4,0},{6,2},{8,12},{10,14},{12,8},{14,10},{16,20},{18,... | collective-permute-start | bytes 417800 | tf_op jit(solution)/shard_map/ppermute | solution.py:50
  27.1 5.8 %collective-permute-start.8 = (bf16[512,1024]{1,0:T(8,128)(2,1)S(1)}, bf16[512,1024]{1,0:T(8,128)(2,1)S(1)}, u32[]{:S(2)}, u32[]{:S(2)}) collective-permute-start(bf16[512,1024]{1,0:T(8,128)(2,1)S(1)} %pad_maximum_fusion.1.refs_8_.refs_0_), channel_id=1, source_target_pairs={{0,1},{1,0},{2,3},{3,2},{4,5},{5,4},{6,7},{7,6},{8,9},{9,8},{10,11... | collective-permute-start | bytes 3145736 | tf_op jit(solution)/shard_map/ppermute | solution.py:50
  31.7 5.1 %collective-permute-start.10 = (bf16[512,1024]{1,0:T(8,128)(2,1)S(1)}, bf16[512,1024]{1,0:T(8,128)(2,1)S(1)}, u32[]{:S(2)}, u32[]{:S(2)}) collective-permute-start(bf16[512,1024]{1,0:T(8,128)(2,1)S(1)} %collective-permute-done.9.refs_0_.refs_1_), channel_id=1, source_target_pairs={{0,1},{1,0},{2,3},{3,2},{4,5},{5,4},{6,7},{7,6},{8,9},{9,8},{10,11... | collective-permute-start | bytes 3145736 | tf_op jit(solution)/shard_map/ppermute | solution.py:50
  31.8 6.9 %collective-permute-start.13 = (bf16[512,128]{1,0:T(8,128)(2,1)S(1)}, bf16[512,128]{1,0:T(8,128)(2,1)S(1)}, u32[]{:S(2)}, u32[]{:S(2)}) collective-permute-start(bf16[512,128]{1,0:T(8,128)(2,1)S(1)} %get-tuple-element.186), channel_id=1, source_target_pairs={{0,2},{2,0},{4,6},{6,4},{8,10},{10,8},{12,14},{14,12},{16,18},{18,... | collective-permute-start | bytes 393224 | tf_op jit(solution)/shard_map/ppermute | solution.py:50
  35.8 6.4 %collective-permute-start.12 = (bf16[512,128]{1,0:T(8,128)(2,1)S(1)}, bf16[512,128]{1,0:T(8,128)(2,1)S(1)}, u32[]{:S(2)}, u32[]{:S(2)}) collective-permute-start(bf16[512,128]{1,0:T(8,128)(2,1)S(1)} %get-tuple-element.91), channel_id=1, source_target_pairs={{0,2},{2,0},{4,6},{6,4},{8,10},{10,8},{12,14},{14,12},{16,18},{18,... | collective-permute-start | bytes 393224 | tf_op jit(solution)/shard_map/ppermute | solution.py:50
  37.6 7.4 %collective-permute-start.11 = (bf16[512,128]{1,0:T(8,128)(2,1)S(1)}, bf16[512,128]{1,0:T(8,128)(2,1)S(1)}, u32[]{:S(2)}, u32[]{:S(2)}) collective-permute-start(bf16[512,128]{1,0:T(8,128)(2,1)S(1)} %get-tuple-element.89), channel_id=1, source_target_pairs={{0,2},{2,0},{4,6},{6,4},{8,10},{10,8},{12,14},{14,12},{16,18},{18,... | collective-permute-start | bytes 393224 | tf_op jit(solution)/shard_map/ppermute | solution.py:50
  38.7 12.4 %collective-permute-start.16 = (bf16[512,128]{1,0:T(8,128)(2,1)S(1)}, bf16[512,128]{1,0:T(8,128)(2,1)S(1)}, u32[]{:S(2)}, u32[]{:S(2)}) collective-permute-start(bf16[512,128]{1,0:T(8,128)(2,1)S(1)} %get-tuple-element.182), channel_id=1, source_target_pairs={{0,2},{2,0},{4,6},{6,4},{8,10},{10,8},{12,14},{14,12},{16,18},{18,... | collective-permute-start | bytes 393224 | tf_op jit(solution)/shard_map/ppermute | solution.py:50
  45.3 4.1 %collective-permute-start.14 = (bf16[128,128]{1,0:T(8,128)(2,1)S(1)}, bf16[128,128]{1,0:T(8,128)(2,1)S(1)}, u32[]{:S(2)}, u32[]{:S(2)}) collective-permute-start(bf16[128,128]{1,0:T(8,128)(2,1)S(1)} %get-tuple-element.96), channel_id=1, source_target_pairs={{0,4},{2,6},{4,0},{6,2},{8,12},{10,14},{12,8},{14,10},{16,20},{18,... | collective-permute-start | bytes 98312 | tf_op jit(solution)/shard_map/ppermute | solution.py:50
  46.1 5.0 %collective-permute-start.17 = (bf16[512,128]{1,0:T(8,128)(2,1)S(1)}, bf16[512,128]{1,0:T(8,128)(2,1)S(1)}, u32[]{:S(2)}, u32[]{:S(2)}) collective-permute-start(bf16[512,128]{1,0:T(8,128)(2,1)S(1)} %get-tuple-element.178), channel_id=1, source_target_pairs={{0,2},{2,0},{4,6},{6,4},{8,10},{10,8},{12,14},{14,12},{16,18},{18,... | collective-permute-start | bytes 393224 | tf_op jit(solution)/shard_map/ppermute | solution.py:50
  53.5 4.9 %collective-permute-start.18 = (bf16[128,128]{1,0:T(8,128)(2,1)S(1)}, bf16[128,128]{1,0:T(8,128)(2,1)S(1)}, u32[]{:S(2)}, u32[]{:S(2)}) collective-permute-start(bf16[128,128]{1,0:T(8,128)(2,1)S(1)} %fusion.2), channel_id=1, source_target_pairs={{0,16},{2,18},{4,20},{6,22},{8,24},{10,26},{12,28},{14,30},{16,0},... | collective-permute-start | bytes 98312 | tf_op jit(solution)/shard_map/ppermute | solution.py:50
  59.1 4.2 %collective-permute-start.19 = (bf16[128,128]{1,0:T(8,128)(2,1)S(1)}, bf16[128,128]{1,0:T(8,128)(2,1)S(1)}, u32[]{:S(2)}, u32[]{:S(2)}) collective-permute-start(bf16[128,128]{1,0:T(8,128)(2,1)S(1)} %get-tuple-element.114), channel_id=1, source_target_pairs={{0,4},{2,6},{4,0},{6,2},{8,12},{10,14},{12,8},{14,10},{16,20},{18,... | collective-permute-start | bytes 98312 | tf_op jit(solution)/shard_map/ppermute | solution.py:50
  60.3 6.5 %collective-permute-start.21 = (bf16[512,128]{1,0:T(8,128)(2,1)S(1)}, bf16[512,128]{1,0:T(8,128)(2,1)S(1)}, u32[]{:S(2)}, u32[]{:S(2)}) collective-permute-start(bf16[512,128]{1,0:T(8,128)(2,1)S(1)} %get-tuple-element.174), channel_id=1, source_target_pairs={{0,2},{2,0},{4,6},{6,4},{8,10},{10,8},{12,14},{14,12},{16,18},{18,... | collective-permute-start | bytes 393224 | tf_op jit(solution)/shard_map/ppermute | solution.py:50
  63.4 4.5 %collective-permute-start.20 = (bf16[128,128]{1,0:T(8,128)(2,1)S(1)}, bf16[128,128]{1,0:T(8,128)(2,1)S(1)}, u32[]{:S(2)}, u32[]{:S(2)}) collective-permute-start(bf16[128,128]{1,0:T(8,128)(2,1)S(1)} %fusion.8), channel_id=1, source_target_pairs={{0,8},{2,10},{4,12},{6,14},{8,0},{10,2},{12,4},{14,6},{16,24},{18,... | collective-permute-start | bytes 98312 | tf_op jit(solution)/shard_map/ppermute | solution.py:50
  66.8 6.4 %collective-permute-start.23 = (bf16[1024,128]{1,0:T(8,128)(2,1)S(1)}, bf16[1024,128]{1,0:T(8,128)(2,1)S(1)}, u32[]{:S(2)}, u32[]{:S(2)}) collective-permute-start(bf16[1024,128]{1,0:T(8,128)(2,1)S(1)} %get-tuple-element.128), channel_id=1, source_target_pairs={{0,2},{2,0},{4,6},{6,4},{8,10},{10,8},{12,14},{14,12},{16,18},{18,... | collective-permute-start | bytes 786440 | tf_op jit(solution)/shard_map/ppermute | solution.py:50
  67.9 4.9 %collective-permute-start.22 = (bf16[128,128]{1,0:T(8,128)(2,1)S(1)}, bf16[128,128]{1,0:T(8,128)(2,1)S(1)}, u32[]{:S(2)}, u32[]{:S(2)}) collective-permute-start(bf16[128,128]{1,0:T(8,128)(2,1)S(1)} %fusion.6), channel_id=1, source_target_pairs={{0,16},{2,18},{4,20},{6,22},{8,24},{10,26},{12,28},{14,30},{16,0},... | collective-permute-start | bytes 98312 | tf_op jit(solution)/shard_map/ppermute | solution.py:50
  73.2 4.3 %collective-permute-start.24 = (bf16[128,128]{1,0:T(8,128)(2,1)S(1)}, bf16[128,128]{1,0:T(8,128)(2,1)S(1)}, u32[]{:S(2)}, u32[]{:S(2)}) collective-permute-start(bf16[128,128]{1,0:T(8,128)(2,1)S(1)} %fusion.5.after_ref), channel_id=1, source_target_pairs={{0,2},{2,0},{4,6},{6,4},{8,10},{10,8},{12,14},{14,12},{16,18},{18,... | collective-permute-start | bytes 98312 | tf_op jit(solution)/shard_map/ppermute | solution.py:50
  78.9 11.6 %collective-permute-start.25 = (bf16[3,512,128]{2,1,0:T(8,128)(2,1)S(1)}, bf16[3,512,128]{2,1,0:T(8,128)(2,1)S(1)}, u32[]{:S(2)}, u32[]{:S(2)}) collective-permute-start(bf16[3,512,128]{2,1,0:T(8,128)(2,1)S(1)} %pad_maximum_fusion.2), channel_id=1, source_target_pairs={{0,2},{2,0},{4,6},{6,4},{8,10},{10,8},{12,14},{14,12},{16,18},{18,... | collective-permute-start | bytes 1179656 | tf_op jit(solution)/shard_map/ppermute | solution.py:50
  80.0 5.0 %collective-permute-start.27 = (bf16[256,256]{1,0:T(8,128)(2,1)S(1)}, bf16[256,256]{1,0:T(8,128)(2,1)S(1)}, u32[]{:S(2)}, u32[]{:S(2)}) collective-permute-start(bf16[256,256]{1,0:T(8,128)(2,1)S(1)} %get-tuple-element.166), channel_id=1, source_target_pairs={{0,4},{2,6},{4,0},{6,2},{8,12},{10,14},{12,8},{14,10},{16,20},{18,... | collective-permute-start | bytes 393224 | tf_op jit(solution)/shard_map/ppermute | solution.py:50
  80.9 7.5 %collective-permute-start.29 = (bf16[256,256]{1,0:T(8,128)(2,1)S(1)}, bf16[256,256]{1,0:T(8,128)(2,1)S(1)}, u32[]{:S(2)}, u32[]{:S(2)}) collective-permute-start(bf16[256,256]{1,0:T(8,128)(2,1)S(1)} %get-tuple-element.165), channel_id=1, source_target_pairs={{0,4},{2,6},{4,0},{6,2},{8,12},{10,14},{12,8},{14,10},{16,20},{18,... | collective-permute-start | bytes 393224 | tf_op jit(solution)/shard_map/ppermute | solution.py:50
  82.1 6.9 %collective-permute-start.31 = (bf16[256,256]{1,0:T(8,128)(2,1)S(1)}, bf16[256,256]{1,0:T(8,128)(2,1)S(1)}, u32[]{:S(2)}, u32[]{:S(2)}) collective-permute-start(bf16[256,256]{1,0:T(8,128)(2,1)S(1)} %get-tuple-element.164), channel_id=1, source_target_pairs={{0,4},{2,6},{4,0},{6,2},{8,12},{10,14},{12,8},{14,10},{16,20},{18,... | collective-permute-start | bytes 393224 | tf_op jit(solution)/shard_map/ppermute | solution.py:50
  82.9 9.8 %collective-permute-start.26 = (bf16[256,256]{1,0:T(8,128)(2,1)S(1)}, bf16[256,256]{1,0:T(8,128)(2,1)S(1)}, u32[]{:S(2)}, u32[]{:S(2)}) collective-permute-start(bf16[256,256]{1,0:T(8,128)(2,1)S(1)} %get-tuple-element.167), channel_id=1, source_target_pairs={{0,4},{2,6},{4,0},{6,2},{8,12},{10,14},{12,8},{14,10},{16,20},{18,... | collective-permute-start | bytes 393224 | tf_op jit(solution)/shard_map/ppermute | solution.py:50
  85.1 10.4 %collective-permute-start.28 = (bf16[256,256]{1,0:T(8,128)(2,1)S(1)}, bf16[256,256]{1,0:T(8,128)(2,1)S(1)}, u32[]{:S(2)}, u32[]{:S(2)}) collective-permute-start(bf16[256,256]{1,0:T(8,128)(2,1)S(1)} %shard_map.95), channel_id=1, source_target_pairs={{0,24},{2,26},{4,28},{6,30},{8,16},{10,18},{12,20},{14,22},{16,8},... | collective-permute-start | bytes 393224 | tf_op jit(solution)/shard_map/ppermute | solution.py:50
  88.4 7.1 %collective-permute-start.30 = (bf16[256,256]{1,0:T(8,128)(2,1)S(1)}, bf16[256,256]{1,0:T(8,128)(2,1)S(1)}, u32[]{:S(2)}, u32[]{:S(2)}) collective-permute-start(bf16[256,256]{1,0:T(8,128)(2,1)S(1)} %shard_map.96), channel_id=1, source_target_pairs={{0,16},{2,18},{4,20},{6,22},{8,24},{10,26},{12,28},{14,30},{16,0},... | collective-permute-start | bytes 393224 | tf_op jit(solution)/shard_map/ppermute | solution.py:50
  89.1 6.4 %collective-permute-start.32 = (bf16[256,256]{1,0:T(8,128)(2,1)S(1)}, bf16[256,256]{1,0:T(8,128)(2,1)S(1)}, u32[]{:S(2)}, u32[]{:S(2)}) collective-permute-start(bf16[256,256]{1,0:T(8,128)(2,1)S(1)} %shard_map.97), channel_id=1, source_target_pairs={{0,8},{2,10},{4,12},{6,14},{8,0},{10,2},{12,4},{14,6},{16,24},{18,... | collective-permute-start | bytes 393224 | tf_op jit(solution)/shard_map/ppermute | solution.py:50
  (17 other events, 209.7 us)
